TPU v7x, 512 devices: a whole 4x8x8 slice. The times are simulated.
512 devices in a mesh: gx: 8 (over z_lo, x), gy: 4 (over z_hi), gz: 16 (over y, core).
Axes of the slice: x: 4, y: 8, z: 8 (z_hi: 4, z_lo: 2; z = z_hi * 2 + z_lo), core: 2. Of those that a mesh axis runs over, the one named last changes fastest.
Arguments:
- body_load: float32 [3, 32, 64, 2048], P(None, 'gx', 'gy', 'gz'), may hold values from -24 to 24
- contact_mask: int32 [32, 64, 2048], P('gx', 'gy', 'gz'), may hold values 0 or 1
- contact_gap: float32 [32, 64, 2048], P('gx', 'gy', 'gz'), may hold values from 0.1 to 0.8
- material_ids: int32 [32, 64, 2048], P('gx', 'gy', 'gz'), may hold values from 0 to 3
- lame_table: float32 [4, 2], replicated, may hold values from 0.5 to 2
Outputs:
- displacement: float32 [3, 32, 64, 2048], P(None, 'gx', 'gy', 'gz')
- multiplier: float32 [3, 32, 64, 2048], P(None, 'gx', 'gy', 'gz')
- gap_history: float32 [6], replicated
All inputs are finite; a program needn't handle non-finite values. No bound on the sum of `contact_mask` on one device may be relied on, other than what follows from the above.
Results may differ from a plain program's by a relative error of at most 0.0001.
Values sent between devices are 32-bit elements; how exact they have to be, the bound alone decides.
No kernel may reach another device: no remote copies, remote signals or barrier semaphores. Data moves between devices by JAX's collectives and lax.ppermute only.
A program may use at most 64 MiB of HBM per device.

v0:
```python
import jax
import jax.numpy as jnp
import numpy as np
from jax import lax
from jax.experimental import pallas as pl
from jax.experimental.pallas import tpu as pltpu
from jax.sharding import PartitionSpec as P

ITERS = 6
DEPTH = ITERS - 1
SWAP = ("gy", "gx")
CHUNK = 4
WIDE = CHUNK + 2 * DEPTH
SLOT = 40
BACK = 16
LOWEST = float(np.finfo(np.float32).min)


def corner_offsets(a):
    return (a >> 2 & 1, a >> 1 & 1, a & 1)


def element_tables():
    points = np.array([(1.0 - 3.0 ** (-0.5)) / 2.0, (1.0 + 3.0 ** (-0.5)) / 2.0])
    stiff_lame = np.zeros((24, 24))
    stiff_shear = np.zeros((24, 24))
    for p in points:
        for q in points:
            for r in points:
                position = (p, q, r)
                gradients = np.zeros((8, 3))
                for a in range(8):
                    corner = corner_offsets(a)
                    for d in range(3):
                        factor = 1.0
                        for e in range(3):
                            if e == d:
                                factor = factor * (1.0 if corner[e] else -1.0)
                            else:
                                factor = factor * (position[e] if corner[e] else 1.0 - position[e])
                        gradients[a, d] = factor
                for a in range(8):
                    for c in range(3):
                        for b in range(8):
                            for d in range(3):
                                stiff_lame[3 * a + c, 3 * b + d] += (
                                    0.125 * gradients[a, c] * gradients[b, d]
                                )
                                stiff_shear[3 * a + c, 3 * b + d] += 0.125 * (
                                    float(c == d) * np.dot(gradients[a], gradients[b])
                                    + gradients[a, d] * gradients[b, c]
                                )
    return (stiff_lame, stiff_shear)


def bounds():
    stiff_lame, stiff_shear = element_tables()
    return (
        float(np.max(np.sum(np.abs(stiff_lame), 1))),
        float(np.max(np.sum(np.abs(stiff_shear), 1))),
    )


def turn_kernel(load_ref, mask_ref, gap_ref, ids_ref, rows_ref, first_ref, last_ref):
    flat = lambda v: v.reshape(64, 128)
    low = jnp.where(mask_ref[...] > 0, -gap_ref[...], LOWEST)
    low = flat(low)
    ids = flat(ids_ref[...].astype(jnp.float32))
    pairs = (
        (flat(load_ref[0]), flat(load_ref[1])),
        (flat(load_ref[2]), ids),
        (low, low),
    )
    for i, pair in enumerate(pairs):
        turned = jnp.concatenate(pair, 0).T
        rows_ref[i] = turned
        first_ref[i] = turned[:8]
        last_ref[i] = turned[120:]


def slots_kernel(rows_ref, before_ref, after_ref, out_ref, wide):
    for i in range(3):
        wide[i, 0:8] = before_ref[i]
        wide[i, 8:136] = rows_ref[i]
        wide[i, 136:144] = after_ref[i]
    lower = lax.broadcasted_iota(jnp.int32, (6, 128), 1) < 64
    for d in range(32):
        at = CHUNK * d + 8 - DEPTH
        out_ref[d, 0:WIDE] = wide[0, at : at + WIDE]
        out_ref[d, 16 : 16 + WIDE] = wide[1, at : at + WIDE]
        out_ref[d, 32:38] = jnp.where(
            lower, wide[2, at + 1 : at + 7], wide[2, at + 7 : at + 13]
        )


def flip(v, even):
    return jnp.where(even, pltpu.roll(v, 7, 0), pltpu.roll(v, 1, 0))


def make_shifts():
    lane = lax.broadcasted_iota(jnp.int32, (8, 128), 1)
    even = lax.broadcasted_iota(jnp.int32, (8, 128), 0) % 2 == 0
    top_x, low_x = lane >= 112, lane < 16
    top_y, low_y = lane % 16 == 15, lane % 16 == 0

    def x_up(v):
        r0, r1 = pltpu.roll(v[0], 112, 1), pltpu.roll(v[1], 112, 1)
        return (jnp.where(top_x, r1, r0), jnp.where(top_x, flip(r0, even), r1))

    def x_down(v):
        r0, r1 = pltpu.roll(v[0], 16, 1), pltpu.roll(v[1], 16, 1)
        return (jnp.where(low_x, flip(r1, even), r0), jnp.where(low_x, r0, r1))

    def y_up(v):
        return tuple(
            jnp.where(top_y, pltpu.roll(pltpu.roll(a, 6, 0), 15, 1), pltpu.roll(a, 127, 1))
            for a in v
        )

    def y_down(v):
        return tuple(
            jnp.where(low_y, pltpu.roll(pltpu.roll(a, 2, 0), 113, 1), pltpu.roll(a, 1, 1))
            for a in v
        )

    return (x_up, x_down, y_up, y_down)


def add(a, b):
    return tuple(i + j for i, j in zip(a, b))


def sub(a, b):
    return tuple(i - j for i, j in zip(a, b))


def element(low, high, lam, mu):
    s = [[h + l for l, h in zip(low[c], high[c])] for c in range(3)]
    d = [[h - l for l, h in zip(low[c], high[c])] for c in range(3)]
    lam3, mu3, mu2 = lam * (1.0 / 3.0), mu * (1.0 / 3.0), mu + mu
    last = (lam + 4.0 * mu) * (1.0 / 9.0)
    SS, DS, SD, DD = range(4)
    fs = [[None] * 4 for _ in range(3)]
    fd = [[None] * 4 for _ in range(3)]
    exx, eyy, ezz = s[0][DS], s[1][SD], d[2][SS]
    trace = lam * (exx + eyy + ezz)
    fs[0][DS] = trace + mu2 * exx
    fs[1][SD] = trace + mu2 * eyy
    fd[2][SS] = trace + mu2 * ezz
    fs[0][SD] = fs[1][DS] = mu * (s[0][SD] + s[1][DS])
    fd[0][SS] = fs[2][DS] = mu * (d[0][SS] + s[2][DS])
    fd[1][SS] = fs[2][SD] = mu * (d[1][SS] + s[2][SD])
    both = lam3 * (s[0][DD] + d[2][SD])
    fs[0][DD] = both + mu * s[0][DD]
    fd[2][SD] = both + mu * d[2][SD]
    both = lam3 * (s[1][DD] + d[2][DS])
    fs[1][DD] = both + mu * s[1][DD]
    fd[2][DS] = both + mu * d[2][DS]
    both = lam3 * (d[0][DS] + d[1][SD])
    fd[0][DS] = both + mu * d[0][DS]
    fd[1][SD] = both + mu * d[1][SD]
    total = s[2][DD] + d[1][DS] + d[0][SD]
    fs[2][DD] = mu3 * (total + s[2][DD])
    fd[1][DS] = mu3 * (total + d[1][DS])
    fd[0][SD] = mu3 * (total + d[0][SD])
    for c in range(3):
        fd[c][DD] = last * d[c][DD]
    down = [[-fd[c][0]] + [fs[c][m] - fd[c][m] for m in (1, 2, 3)] for c in range(3)]
    up = [[fd[c][0]] + [fs[c][m] + fd[c][m] for m in (1, 2, 3)] for c in range(3)]
    return (down, up)


def iterate_kernel(gl, gm, table_ref, in_ref, out_ref, u, u1, quad, dual, low, lam, mu, modes, forces):
    lane = lax.broadcasted_iota(jnp.int32, (8, 128), 1)
    left = lane < 64
    x_up, x_down, y_up, y_down = make_shifts()
    weight = jnp.full((8, 128), table_ref[0, 0] * gl + table_ref[0, 1] * gm, jnp.float32)
    for m in range(1, 4):
        weight = jnp.maximum(weight, table_ref[m, 0] * gl + table_ref[m, 1] * gm)
    step = 1.5 / (1.0 + 8.0 * weight)
    scale = step * (1.0 / 16.0)
    lams = [scale * table_ref[m, 0] for m in range(4)]
    mus = [scale * table_ref[m, 1] for m in range(4)]

    def fetch(row, v):
        even = in_ref[pl.ds(2 * v * SLOT + row, 8, stride=4 * SLOT), :]
        odd = in_ref[pl.ds((2 * v + 1) * SLOT + row, 8, stride=4 * SLOT), :]
        return (
            jnp.where(left, even, pltpu.roll(odd, 64, 1)),
            jnp.where(left, pltpu.roll(even, 64, 1), odd),
        )

    peak = []
    for p in range(WIDE):
        for v in range(2):
            b0, b1 = fetch(p, v)
            b2, ids = fetch(16 + p, v)
            for c, b in enumerate((b0, b1, b2)):
                b = step * b
                u[c, p, v] = b
                u1[c, p, v] = b
            if p < WIDE - 1:
                first, shear = lams[0], mus[0]
                for m in range(1, 4):
                    hit = ids == float(m)
                    first = jnp.where(hit, lams[m], first)
                    shear = jnp.where(hit, mus[m], shear)
                lam[p, v] = first
                mu[p, v] = shear
    for k in range(6):
        for v in range(2):
            near, far = fetch(32 + k, v)
            low[1 + k, v] = near
            low[7 + k, v] = far

    def project(p, v, new, old, own):
        shifted = new if old is None else new + old
        z = jnp.maximum(shifted, low[p, v])
        now = shifted - z
        dual[p, v] = now
        apart = new - z
        quad[p, v] = step * (apart + now)
        if own:
            peak.append(jnp.abs(apart))

    def largest():
        top = peak[0]
        for a in peak[1:]:
            top = jnp.maximum(top, a)
        peak.clear()
        top = jnp.max(top, axis=1, keepdims=True)
        return jnp.max(top, axis=0, keepdims=True)

    mine = range(DEPTH, DEPTH + CHUNK)
    for p in range(1, WIDE - 1):
        for v in range(2):
            project(p, v, u[2, p, v], None, p in mine)
    history = [largest()]
    for t in range(1, ITERS):
        lo, hi = t, WIDE - 1 - t
        for p in range(lo - 1, hi + 2):
            for c in range(3):
                value = (u[c, p, 0], u[c, p, 1])
                other = y_up(value)
                ys, yd = add(other, value), sub(other, value)
                for m, part in ((0, ys), (2, yd)):
                    other = x_up(part)
                    xs, xd = add(other, part), sub(other, part)
                    for v in range(2):
                        modes[c, m, p, v] = xs[v]
                        modes[c, m + 1, p, v] = xd[v]
        for v in range(2):
            held = None
            below = [[modes[c, m, lo - 1, v] for m in range(4)] for c in range(3)]
            for e in range(lo - 1, hi + 1):
                above = [[modes[c, m, e + 1, v] for m in range(4)] for c in range(3)]
                down, up = element(below, above, lam[e, v], mu[e, v])
                if held is not None:
                    for c in range(3):
                        for m in range(4):
                            forces[c, m, e, v] = held[c][m] + down[c][m]
                held, below = up, above
        for p in range(lo, hi + 1):
            for c in range(3):
                f = [(forces[c, m, p, 0], forces[c, m, p, 1]) for m in range(4)]
                ys = add(sub(f[0], f[1]), x_down(add(f[0], f[1])))
                yd = add(sub(f[2], f[3]), x_down(add(f[2], f[3])))
                total = add(sub(ys, yd), y_down(add(ys, yd)))
                for v in range(2):
                    new = u[c, p, v] - total[v] + u1[c, p, v]
                    if c == 2:
                        new = new - quad[p, v]
                        project(p, v, new, dual[p, v], p in mine)
                    u[c, p, v] = new
        history.append(largest())
    gaps = jnp.zeros((8, 128), jnp.float32)
    for t, top in enumerate(history):
        gaps = jnp.where(lane == t, top, gaps)
    for k, p in enumerate(mine):
        for v in range(2):
            for row, a, b in (
                (k, u[0, p, v], u[1, p, v]),
                (CHUNK + k, u[2, p, v], dual[p, v]),
            ):
                even = jnp.where(left, a, pltpu.roll(b, 64, 1))
                odd = jnp.where(left, pltpu.roll(a, 64, 1), b)
                out_ref[pl.ds(2 * v * BACK + row, 8, stride=4 * BACK), :] = even
                out_ref[pl.ds((2 * v + 1) * BACK + row, 8, stride=4 * BACK), :] = odd
    for i in range(4):
        out_ref[pl.ds(i * BACK + 8, 8, stride=4 * BACK), :] = gaps


def bricks_kernel(in_ref, u_ref, w_ref, gaps_ref, rows):
    top = jnp.max(in_ref[:, 8, :], axis=0, keepdims=True)
    gaps_ref[...] = jnp.broadcast_to(top[None], gaps_ref.shape)
    for d in range(32):
        rows[0, CHUNK * d : CHUNK * d + CHUNK] = in_ref[d, 0:CHUNK]
        rows[1, CHUNK * d : CHUNK * d + CHUNK] = in_ref[d, CHUNK : 2 * CHUNK]
    brick = u_ref.shape[1:]
    first = rows[0].T
    u_ref[0] = first[:64].reshape(brick)
    u_ref[1] = first[64:].reshape(brick)
    second = rows[1].T
    u_ref[2] = second[:64].reshape(brick)
    w_ref[0] = jnp.zeros(brick, jnp.float32)
    w_ref[1] = jnp.zeros(brick, jnp.float32)
    w_ref[2] = second[64:].reshape(brick)


def shards(body_load, contact_mask, contact_gap, material_ids, lame_table):
    f32 = jnp.float32
    params = pltpu.CompilerParams(vmem_limit_bytes=32 * 1024 * 1024)
    shape = lambda *dims: jax.ShapeDtypeStruct(dims, f32)
    vmem = pl.BlockSpec(memory_space=pltpu.VMEM)
    smem = pl.BlockSpec(memory_space=pltpu.SMEM)
    rows, first, last = pl.pallas_call(
        turn_kernel,
        out_shape=(shape(3, 128, 128), shape(3, 8, 128), shape(3, 8, 128)),
        in_specs=[vmem] * 4,
        out_specs=(vmem,) * 3,
        compiler_params=params,
        name="turn",
    )(body_load, contact_mask, contact_gap, material_ids)
    count = lax.axis_size("gz")
    before = lax.ppermute(last, "gz", [(i, (i + 1) % count) for i in range(count)])
    after = lax.ppermute(first, "gz", [(i, (i - 1) % count) for i in range(count)])
    slots = pl.pallas_call(
        slots_kernel,
        out_shape=shape(32, SLOT, 128),
        in_specs=[vmem] * 3,
        out_specs=vmem,
        scratch_shapes=[pltpu.VMEM((3, 144, 128), f32)],
        compiler_params=params,
        name="slots",
    )(rows, before, after)
    slots = lax.all_to_all(slots, SWAP, 0, 0, tiled=True)
    gl, gm = bounds()
    back = pl.pallas_call(
        lambda *refs: iterate_kernel(gl, gm, *refs),
        out_shape=shape(32 * BACK, 128),
        in_specs=[smem, vmem],
        out_specs=vmem,
        scratch_shapes=[
            pltpu.VMEM((3, WIDE, 2, 8, 128), f32),
            pltpu.VMEM((3, WIDE, 2, 8, 128), f32),
            pltpu.VMEM((WIDE, 2, 8, 128), f32),
            pltpu.VMEM((WIDE, 2, 8, 128), f32),
            pltpu.VMEM((WIDE, 2, 8, 128), f32),
            pltpu.VMEM((WIDE, 2, 8, 128), f32),
            pltpu.VMEM((WIDE, 2, 8, 128), f32),
            pltpu.VMEM((3, 4, WIDE, 2, 8, 128), f32),
            pltpu.VMEM((3, 4, WIDE, 2, 8, 128), f32),
        ],
        compiler_params=params,
        name="iterate",
    )(lame_table, slots.reshape(32 * SLOT, 128))
    back = lax.all_to_all(back.reshape(32, BACK, 128), SWAP, 0, 0, tiled=True)
    displacement, multiplier, gaps = pl.pallas_call(
        bricks_kernel,
        out_shape=(shape(*body_load.shape), shape(*body_load.shape), shape(count, 8, 128)),
        in_specs=[vmem],
        out_specs=(vmem,) * 3,
        scratch_shapes=[pltpu.VMEM((2, 128, 128), f32)],
        compiler_params=params,
        name="bricks",
    )(back)
    gaps = lax.all_to_all(gaps, "gz", 0, 0, tiled=True)
    return (displacement, multiplier, jnp.max(gaps[:, 0, :ITERS], axis=0))


def solution(mesh):
    node, field = P("gx", "gy", "gz"), P(None, "gx", "gy", "gz")
    return jax.shard_map(
        shards,
        mesh=mesh,
        in_specs=(field, node, node, node, P()),
        out_specs=(field, field, P()),
        check_vma=False,
    )
```

profile of v0, /device:TPU:1, one launch (start us, length us, event | category | flops | bytes accessed | tf_op | source)
XLA Modules:
  0.0 98.2 jit_solution(16389143373858725466)
XLA Ops:
  0.6 0.0 copy-start
  0.6 0.9 copy-done
  1.5 0.0 copy-start.1
  1.5 0.8 copy-done.1
  2.3 0.0 copy-start.2
  2.3 0.8 copy-done.2
  3.0 0.0 copy-start.3
  3.0 0.8 copy-done.3
  3.8 0.1 turn.1
  3.9 2.7 %collective-permute-start = (f32[3,8,128]{2,1,0:T(8,128)S(1)}, f32[3,8,128]{2,1,0:T(8,128)S(1)}, u32[]{:S(2)}, u32[]{:S(2)}) collective-permute-start(f32[3,8,128]{2,1,0:T(8,128)S(1)} %get-tuple-element.10), channel_id=1, source_target_pairs={{0,1},{1,2},{2,3},{3,4},{4,5},{5,6},{6,7},{7,8},{8,9},{9,10},{10,1... | collective-permute-start | bytes 36872 | tf_op jit(solution)/shard_map/ppermute | solution.py:325
  6.6 4.2 %collective-permute-start.1 = (f32[3,8,128]{2,1,0:T(8,128)S(1)}, f32[3,8,128]{2,1,0:T(8,128)S(1)}, u32[]{:S(2)}, u32[]{:S(2)}) collective-permute-start(f32[3,8,128]{2,1,0:T(8,128)S(1)} %get-tuple-element.11), channel_id=1, source_target_pairs={{0,15},{1,0},{2,1},{3,2},{4,3},{5,4},{6,5},{7,6},{8,7},{9,8},{10,9... | collective-permute-start | bytes 36872 | tf_op jit(solution)/shard_map/ppermute | solution.py:326
  10.8 0.6 collective-permute-done.before_ref
  11.5 0.2 collective-permute-done.1.after_ref
  11.7 0.9 slots.1
  12.6 0.0 copy-start.4
  12.6 11.1 %all-to-all-start = ((f32[32,40,128]{2,1,0:T(8,128)}), f32[32,40,128]{2,1,0:T(8,128)S(1)}, u32[]{:S(2)}, u32[]{:S(2)}) async-start(f32[32,40,128]{2,1,0:T(8,128)} %slots.1), calls=%async_computation | async-start | bytes 1310720 | tf_op jit(solution)/shard_map/all_to_all | solution.py:336
  23.7 0.0 copy-done.4
  23.7 0.1 copy.8.refs_0_
  23.8 19.1 %all-to-all-done = f32[32,40,128]{2,1,0:T(8,128)S(1)} async-done(((f32[32,40,128]{2,1,0:T(8,128)}), f32[32,40,128]{2,1,0:T(8,128)S(1)}, u32[]{:S(2)}, u32[]{:S(2)}) %all-to-all-start) | async-done | bytes 655392 | tf_op jit(solution)/shard_map/all_to_all | solution.py:336
  42.9 20.9 %iterate.1 = f32[512,128]{1,0:T(8,128)S(1)} custom-call(f32[4,2]{1,0:T(4,128)S(1)} %copy.8.refs_0_, f32[1280,128]{1,0:T(8,128)S(1)} %bitcast.2), custom_call_target="tpu_custom_call" | custom-call | tf_op jit(solution)/shard_map/iterate/pallas_call | solution.py:338
  63.8 15.6 %all_to_all.15.in_ref = f32[32,16,128]{2,1,0:T(8,128)S(1)} all-to-all(f32[32,16,128]{2,1,0:T(8,128)S(1)} %bitcast.3), channel_id=1, replica_groups=mesh['gx'=8,'gy'=4,'gz'=16] {'gy','gx'}, dimensions={0} | all-to-all | bytes 524288 | tf_op jit(solution)/shard_map/all_to_all | solution.py:357
  79.3 0.8 bricks.1
  80.1 17.5 %all_to_all.16 = f32[16,8,128]{2,1,0:T(8,128)S(1)} all-to-all(f32[16,8,128]{2,1,0:T(8,128)S(1)} %get-tuple-element.14), channel_id=1, replica_groups=mesh['gx'=8,'gy'=4,'gz'=16] {'gz'}, dimensions={0} | all-to-all | bytes 131072 | tf_op jit(solution)/shard_map/all_to_all | solution.py:367
  97.7 0.5 slice_reduce_fusion
Async XLA Ops:
  0.6 0.9 copy-start
  1.5 0.8 copy-start.1
  2.3 0.8 copy-start.2
  3.0 0.8 copy-start.3
  3.9 7.6 %collective-permute-start = (f32[3,8,128]{2,1,0:T(8,128)S(1)}, f32[3,8,128]{2,1,0:T(8,128)S(1)}, u32[]{:S(2)}, u32[]{:S(2)}) collective-permute-start(f32[3,8,128]{2,1,0:T(8,128)S(1)} %get-tuple-element.10), channel_id=1, source_target_pairs={{0,1},{1,2},{2,3},{3,4},{4,5},{5,6},{6,7},{7,8},{8,9},{9,10},{10,1... | collective-permute-start | bytes 36872 | tf_op jit(solution)/shard_map/ppermute | solution.py:325
  6.6 5.1 %collective-permute-start.1 = (f32[3,8,128]{2,1,0:T(8,128)S(1)}, f32[3,8,128]{2,1,0:T(8,128)S(1)}, u32[]{:S(2)}, u32[]{:S(2)}) collective-permute-start(f32[3,8,128]{2,1,0:T(8,128)S(1)} %get-tuple-element.11), channel_id=1, source_target_pairs={{0,15},{1,0},{2,1},{3,2},{4,3},{5,4},{6,5},{7,6},{8,7},{9,8},{10,9... | collective-permute-start | bytes 36872 | tf_op jit(solution)/shard_map/ppermute | solution.py:326
  12.6 11.1 %copy-start.4 = (f32[4,2]{0,1:T(2,128)S(1)}, f32[4,2]{0,1:T(2,128)}, u32[]{:S(2)}) copy-start(f32[4,2]{0,1:T(2,128)} %param.9) | copy-start | bytes 100
  12.6 30.3 %all-to-all-start = ((f32[32,40,128]{2,1,0:T(8,128)}), f32[32,40,128]{2,1,0:T(8,128)S(1)}, u32[]{:S(2)}, u32[]{:S(2)}) async-start(f32[32,40,128]{2,1,0:T(8,128)} %slots.1), calls=%async_computation | async-start | bytes 1310720 | tf_op jit(solution)/shard_map/all_to_all | solution.py:336
where the time goes:
time: 98.7 us; the launch traced here: 98.2 us
  blocking collectives  33.1 us (34%)
  Pallas kernels  22.7 us (23%)
  waiting for transfers between devices  19.9 us (20%)
  starting transfers between devices  18 us (18%)
  local copies, waits for them, and re-layouts  3.25 us (3%)
    pallas_call x1, Pallas kernels, shards(): pl.pallas_call(lambda *refs: iterate_kernel(gl, gm, *refs), out_shape=sha...  20.9 us
    all_to_all x1, waiting for transfers between devices, shards(): slots = lax.all_to_all(slots, SWAP, 0, 0, tiled=True)  19.1 us
    all_to_all x1, blocking collectives, shards(): gaps = lax.all_to_all(gaps, 'gz', 0, 0, tiled=True)  17.5 us
    all_to_all x1, blocking collectives, shards(): back = lax.all_to_all(back.reshape(32, BACK, 128), SWAP, 0, 0, tiled=True)  15.6 us
    all_to_all x1, starting transfers between devices, shards(): slots = lax.all_to_all(slots, SWAP, 0, 0, tiled=True)  11.1 us
    ppermute x1, starting transfers between devices, shards(): lax.ppermute(first, 'gz', [(i, (i - 1) % count) for i in range(count)])  4.22 us
    unnamed x11, local copies, waits for them, and re-layouts  3.25 us
    ppermute x1, starting transfers between devices, shards(): lax.ppermute(last, 'gz', [(i, (i + 1) % count) for i in range(count)])  2.7 us
  transfers between devices with their start and end apart: 3, of which 3 were waited for; matrix products, arithmetic and copies ran while one was open for 0% of the time, Pallas kernels for 0%

commit v1 on v0

--- a/solution.py
+++ b/solution.py
@@ -13,6 +13,10 @@
 WIDE = CHUNK + 2 * DEPTH
 SLOT = 40
 BACK = 16
+UNROLL = (7, 4)
+GROUPS = (4, 4)
+PAD = 0
+PLANES = WIDE + max(GROUPS)
 LOWEST = float(np.finfo(np.float32).min)
 
 
@@ -170,7 +174,19 @@
     return (down, up)
 
 
-def iterate_kernel(gl, gm, table_ref, in_ref, out_ref, u, u1, quad, dual, low, lam, mu, modes, forces):
+def loop(lo, hi, body, unroll):
+    lax.fori_loop(lo, hi, lambda i, _: body(i), None, unroll=unroll)
+
+
+def planes(lo, hi, group, body):
+    def step(g, _):
+        for j in range(group):
+            body(lo + g * group + j)
+
+    lax.fori_loop(0, -(-(hi - lo) // group), step, None)
+
+
+def iterate_kernel(gl, gm, table_ref, in_ref, out_ref, u, u1, quad, dual, dist, low, lam, mu, modes, forces):
     lane = lax.broadcasted_iota(jnp.int32, (8, 128), 1)
     left = lane < 64
     x_up, x_down, y_up, y_down = make_shifts()
@@ -190,91 +206,108 @@
             jnp.where(left, pltpu.roll(even, 64, 1), odd),
         )
 
-    peak = []
-    for p in range(WIDE):
+    def unpack(k):
+        p = PAD + k
         for v in range(2):
-            b0, b1 = fetch(p, v)
-            b2, ids = fetch(16 + p, v)
+            b0, b1 = fetch(k, v)
+            b2, ids = fetch(16 + k, v)
             for c, b in enumerate((b0, b1, b2)):
                 b = step * b
                 u[c, p, v] = b
                 u1[c, p, v] = b
-            if p < WIDE - 1:
-                first, shear = lams[0], mus[0]
-                for m in range(1, 4):
-                    hit = ids == float(m)
-                    first = jnp.where(hit, lams[m], first)
-                    shear = jnp.where(hit, mus[m], shear)
-                lam[p, v] = first
-                mu[p, v] = shear
+            first, shear = lams[0], mus[0]
+            for m in range(1, 4):
+                hit = ids == float(m)
+                first = jnp.where(hit, lams[m], first)
+                shear = jnp.where(hit, mus[m], shear)
+            lam[p, v] = first
+            mu[p, v] = shear
+
+    loop(0, WIDE, unpack, UNROLL[0])
     for k in range(6):
         for v in range(2):
             near, far = fetch(32 + k, v)
-            low[1 + k, v] = near
-            low[7 + k, v] = far
-
-    def project(p, v, new, old, own):
-        shifted = new if old is None else new + old
-        z = jnp.maximum(shifted, low[p, v])
-        now = shifted - z
-        dual[p, v] = now
-        apart = new - z
-        quad[p, v] = step * (apart + now)
-        if own:
-            peak.append(jnp.abs(apart))
+            low[PAD + 1 + k, v] = near
+            low[PAD + 7 + k, v] = far
+
+    def project(new, old, bound):
+        shifted = new if old is None else add(new, old)
+        z = tuple(jnp.maximum(a, b) for a, b in zip(shifted, bound))
+        now, apart = sub(shifted, z), sub(new, z)
+        return (now, tuple(step * a for a in add(apart, now)), tuple(jnp.abs(a) for a in apart))
+
+    def keep(p, results):
+        for ref, value in zip((dual, quad, dist), results):
+            put(ref, value, p)
 
     def largest():
-        top = peak[0]
-        for a in peak[1:]:
-            top = jnp.maximum(top, a)
-        peak.clear()
-        top = jnp.max(top, axis=1, keepdims=True)
-        return jnp.max(top, axis=0, keepdims=True)
-
-    mine = range(DEPTH, DEPTH + CHUNK)
-    for p in range(1, WIDE - 1):
+        top = dist[mine[0], 0]
+        for p in mine:
+            for v in range(2):
+                top = jnp.maximum(top, dist[p, v])
+        return top
+
+    def pair(ref, *at):
+        return tuple(ref[*at, v] for v in range(2))
+
+    def put(ref, value, *at):
         for v in range(2):
-            project(p, v, u[2, p, v], None, p in mine)
+            ref[*at, v] = value[v]
+
+    def split(value, shift):
+        other = shift(value)
+        return (add(other, value), sub(other, value))
+
+    def forward(p):
+        for c in range(3):
+            for m, part in enumerate(split(pair(u, c, p), y_up)):
+                for k, value in enumerate(split(part, x_up)):
+                    put(modes, value, c, 2 * m + k, p)
+
+    def layer(v):
+        def body(e, carry):
+            held, below = carry
+            above = [[modes[c, m, e + 1, v] for m in range(4)] for c in range(3)]
+            down, up = element(below, above, lam[e, v], mu[e, v])
+            for c in range(3):
+                for m in range(4):
+                    forces[c, m, e, v] = held[c][m] + down[c][m]
+            return (up, above)
+
+        return body
+
+    def first_project(p):
+        keep(p, project(pair(u, 2, p), None, pair(low, p)))
+
+    def merge(s, d, shift):
+        return add(sub(s, d), shift(add(s, d)))
+
+    def backward(p):
+        for c in range(3):
+            f = [pair(forces, c, m, p) for m in range(4)]
+            total = merge(merge(f[0], f[1], x_down), merge(f[2], f[3], x_down), y_down)
+            new = add(sub(pair(u, c, p), total), pair(u1, c, p))
+            if c == 2:
+                new = sub(new, pair(quad, p))
+                keep(p, project(new, pair(dual, p), pair(low, p)))
+            put(u, new, c, p)
+
+    mine = range(PAD + DEPTH, PAD + DEPTH + CHUNK)
+    loop(PAD + 1, PAD + WIDE - 1, first_project, UNROLL[0])
     history = [largest()]
+    zero = jnp.zeros((8, 128), jnp.float32)
     for t in range(1, ITERS):
-        lo, hi = t, WIDE - 1 - t
-        for p in range(lo - 1, hi + 2):
-            for c in range(3):
-                value = (u[c, p, 0], u[c, p, 1])
-                other = y_up(value)
-                ys, yd = add(other, value), sub(other, value)
-                for m, part in ((0, ys), (2, yd)):
-                    other = x_up(part)
-                    xs, xd = add(other, part), sub(other, part)
-                    for v in range(2):
-                        modes[c, m, p, v] = xs[v]
-                        modes[c, m + 1, p, v] = xd[v]
+        lo, hi = PAD + t, PAD + WIDE - 1 - t
+        planes(lo - 1, hi + 2, GROUPS[0], forward)
         for v in range(2):
-            held = None
             below = [[modes[c, m, lo - 1, v] for m in range(4)] for c in range(3)]
-            for e in range(lo - 1, hi + 1):
-                above = [[modes[c, m, e + 1, v] for m in range(4)] for c in range(3)]
-                down, up = element(below, above, lam[e, v], mu[e, v])
-                if held is not None:
-                    for c in range(3):
-                        for m in range(4):
-                            forces[c, m, e, v] = held[c][m] + down[c][m]
-                held, below = up, above
-        for p in range(lo, hi + 1):
-            for c in range(3):
-                f = [(forces[c, m, p, 0], forces[c, m, p, 1]) for m in range(4)]
-                ys = add(sub(f[0], f[1]), x_down(add(f[0], f[1])))
-                yd = add(sub(f[2], f[3]), x_down(add(f[2], f[3])))
-                total = add(sub(ys, yd), y_down(add(ys, yd)))
-                for v in range(2):
-                    new = u[c, p, v] - total[v] + u1[c, p, v]
-                    if c == 2:
-                        new = new - quad[p, v]
-                        project(p, v, new, dual[p, v], p in mine)
-                    u[c, p, v] = new
+            held = [[zero] * 4 for _ in range(3)]
+            lax.fori_loop(lo - 1, hi + 1, layer(v), (held, below), unroll=UNROLL[1])
+        planes(lo, hi + 1, GROUPS[1], backward)
         history.append(largest())
     gaps = jnp.zeros((8, 128), jnp.float32)
     for t, top in enumerate(history):
+        top = jnp.max(jnp.max(top, axis=0, keepdims=True), axis=1, keepdims=True)
         gaps = jnp.where(lane == t, top, gaps)
     for k, p in enumerate(mine):
         for v in range(2):
@@ -341,15 +374,16 @@
         in_specs=[smem, vmem],
         out_specs=vmem,
         scratch_shapes=[
-            pltpu.VMEM((3, WIDE, 2, 8, 128), f32),
-            pltpu.VMEM((3, WIDE, 2, 8, 128), f32),
-            pltpu.VMEM((WIDE, 2, 8, 128), f32),
-            pltpu.VMEM((WIDE, 2, 8, 128), f32),
-            pltpu.VMEM((WIDE, 2, 8, 128), f32),
-            pltpu.VMEM((WIDE, 2, 8, 128), f32),
-            pltpu.VMEM((WIDE, 2, 8, 128), f32),
-            pltpu.VMEM((3, 4, WIDE, 2, 8, 128), f32),
-            pltpu.VMEM((3, 4, WIDE, 2, 8, 128), f32),
+            pltpu.VMEM((3, PLANES, 2, 8, 128), f32),
+            pltpu.VMEM((3, PLANES, 2, 8, 128), f32),
+            pltpu.VMEM((PLANES, 2, 8, 128), f32),
+            pltpu.VMEM((PLANES, 2, 8, 128), f32),
+            pltpu.VMEM((PLANES, 2, 8, 128), f32),
+            pltpu.VMEM((PLANES, 2, 8, 128), f32),
+            pltpu.VMEM((PLANES, 2, 8, 128), f32),
+            pltpu.VMEM((PLANES, 2, 8, 128), f32),
+            pltpu.VMEM((3, 4, PLANES, 2, 8, 128), f32),
+            pltpu.VMEM((3, 4, PLANES, 2, 8, 128), f32),
         ],
         compiler_params=params,
         name="iterate",

time: 98.7 us -> 85.5 us (0.87)
  Pallas kernels: 22.7 us -> 9.53 us
    pallas_call x1, Pallas kernels: 20.9 us -> 7.71 us  [shards(): pl.pallas_call(lambda *refs: iterate_kernel(gl, gm, *refs), out_shape=sha...]
where the time goes in v1:
time: 85.5 us; the launch traced here: 85 us
  blocking collectives  33.1 us (39%)
  waiting for transfers between devices  19.9 us (23%)
  starting transfers between devices  18 us (21%)
  Pallas kernels  9.53 us (11%)
  local copies, waits for them, and re-layouts  3.25 us (4%)
    all_to_all x1, waiting for transfers between devices, shards(): slots = lax.all_to_all(slots, SWAP, 0, 0, tiled=True)  19.1 us
    all_to_all x1, blocking collectives, shards(): gaps = lax.all_to_all(gaps, 'gz', 0, 0, tiled=True)  17.5 us
    all_to_all x1, blocking collectives, shards(): back = lax.all_to_all(back.reshape(32, BACK, 128), SWAP, 0, 0, tiled=True)  15.6 us
    all_to_all x1, starting transfers between devices, shards(): slots = lax.all_to_all(slots, SWAP, 0, 0, tiled=True)  11.1 us
    pallas_call x1, Pallas kernels, shards(): pl.pallas_call(lambda *refs: iterate_kernel(gl, gm, *refs), out_shape=sha...  7.71 us
    ppermute x1, starting transfers between devices, shards(): lax.ppermute(first, 'gz', [(i, (i - 1) % count) for i in range(count)])  4.22 us
    unnamed x11, local copies, waits for them, and re-layouts  3.25 us
    ppermute x1, starting transfers between devices, shards(): lax.ppermute(last, 'gz', [(i, (i + 1) % count) for i in range(count)])  2.7 us
  transfers between devices with their start and end apart: 3, of which 3 were waited for; matrix products, arithmetic and copies ran while one was open for 0% of the time, Pallas kernels for 0%

profile of v1, /device:TPU:1, one launch (start us, length us, event | category | flops | bytes accessed | tf_op | source)
XLA Modules:
  0.0 85.0 jit_solution(11592944561661865603)
XLA Ops:
  0.6 0.0 copy-start
  0.6 0.9 %copy-done = f32[3,4,16,128]{3,2,1,0:T(8,128)S(1)} copy-done((f32[3,4,16,128]{3,2,1,0:T(8,128)S(1)}, f32[3,4,16,128]{3,2,1,0:T(8,128)}, u32[]{:S(2)}) %copy-start) | copy-done | bytes 98328
  1.5 0.0 copy-start.1
  1.5 0.8 copy-done.1
  2.3 0.0 copy-start.2
  2.3 0.8 copy-done.2
  3.0 0.0 copy-start.3
  3.0 0.8 copy-done.3
  3.8 0.1 turn.1
  3.9 2.7 %collective-permute-start = (f32[3,8,128]{2,1,0:T(8,128)S(1)}, f32[3,8,128]{2,1,0:T(8,128)S(1)}, u32[]{:S(2)}, u32[]{:S(2)}) collective-permute-start(f32[3,8,128]{2,1,0:T(8,128)S(1)} %get-tuple-element.10), channel_id=1, source_target_pairs={{0,1},{1,2},{2,3},{3,4},{4,5},{5,6},{6,7},{7,8},{8,9},{9,10},{10,1... | collective-permute-start | bytes 36872 | tf_op jit(solution)/shard_map/ppermute | solution.py:358
  6.6 4.2 %collective-permute-start.1 = (f32[3,8,128]{2,1,0:T(8,128)S(1)}, f32[3,8,128]{2,1,0:T(8,128)S(1)}, u32[]{:S(2)}, u32[]{:S(2)}) collective-permute-start(f32[3,8,128]{2,1,0:T(8,128)S(1)} %get-tuple-element.11), channel_id=1, source_target_pairs={{0,15},{1,0},{2,1},{3,2},{4,3},{5,4},{6,5},{7,6},{8,7},{9,8},{10,9... | collective-permute-start | bytes 36872 | tf_op jit(solution)/shard_map/ppermute | solution.py:359
  10.8 0.6 collective-permute-done.before_ref
  11.5 0.2 collective-permute-done.1.after_ref
  11.7 0.9 %slots.1 = f32[32,40,128]{2,1,0:T(8,128)} custom-call(f32[3,128,128]{2,1,0:T(8,128)S(1)} %get-tuple-element.9.rows_ref, f32[3,8,128]{2,1,0:T(8,128)S(1)} %collective-permute-done.before_ref, f32[3,8,128]{2,1,0:T(8,128)S(1)} %collective-permute-done.1.after_ref), custom_call_target="tpu_custom_call" | custom-call | tf_op jit(solution)/shard_map/slots/pallas_call | solution.py:360
  12.6 0.0 copy-start.4
  12.6 11.1 %all-to-all-start = ((f32[32,40,128]{2,1,0:T(8,128)}), f32[32,40,128]{2,1,0:T(8,128)S(1)}, u32[]{:S(2)}, u32[]{:S(2)}) async-start(f32[32,40,128]{2,1,0:T(8,128)} %slots.1), calls=%async_computation | async-start | bytes 1310720 | tf_op jit(solution)/shard_map/all_to_all | solution.py:369
  23.7 0.0 copy-done.4
  23.7 0.1 copy.8.refs_0_
  23.8 19.1 %all-to-all-done = f32[32,40,128]{2,1,0:T(8,128)S(1)} async-done(((f32[32,40,128]{2,1,0:T(8,128)}), f32[32,40,128]{2,1,0:T(8,128)S(1)}, u32[]{:S(2)}, u32[]{:S(2)}) %all-to-all-start) | async-done | bytes 655392 | tf_op jit(solution)/shard_map/all_to_all | solution.py:369
  42.9 7.7 %iterate.1 = f32[512,128]{1,0:T(8,128)S(1)} custom-call(f32[4,2]{1,0:T(4,128)S(1)} %copy.8.refs_0_, f32[1280,128]{1,0:T(8,128)S(1)} %bitcast.2), custom_call_target="tpu_custom_call" | custom-call | tf_op jit(solution)/shard_map/iterate/pallas_call | solution.py:371
  50.6 15.6 %all_to_all.15.in_ref = f32[32,16,128]{2,1,0:T(8,128)S(1)} all-to-all(f32[32,16,128]{2,1,0:T(8,128)S(1)} %bitcast.3), channel_id=1, replica_groups=mesh['gx'=8,'gy'=4,'gz'=16] {'gy','gx'}, dimensions={0} | all-to-all | bytes 524288 | tf_op jit(solution)/shard_map/all_to_all | solution.py:391
  66.1 0.8 bricks.1
  66.9 17.5 %all_to_all.16 = f32[16,8,128]{2,1,0:T(8,128)S(1)} all-to-all(f32[16,8,128]{2,1,0:T(8,128)S(1)} %get-tuple-element.14), channel_id=1, replica_groups=mesh['gx'=8,'gy'=4,'gz'=16] {'gz'}, dimensions={0} | all-to-all | bytes 131072 | tf_op jit(solution)/shard_map/all_to_all | solution.py:401
  84.5 0.5 slice_reduce_fusion
Async XLA Ops:
  0.6 0.9 %copy-start = (f32[3,4,16,128]{3,2,1,0:T(8,128)S(1)}, f32[3,4,16,128]{3,2,1,0:T(8,128)}, u32[]{:S(2)}) copy-start(f32[3,4,16,128]{3,2,1,0:T(8,128)} %load_ref.1) | copy-start | bytes 294916
  1.5 0.8 copy-start.1
  2.3 0.8 copy-start.2
  3.0 0.8 copy-start.3
  3.9 7.6 %collective-permute-start = (f32[3,8,128]{2,1,0:T(8,128)S(1)}, f32[3,8,128]{2,1,0:T(8,128)S(1)}, u32[]{:S(2)}, u32[]{:S(2)}) collective-permute-start(f32[3,8,128]{2,1,0:T(8,128)S(1)} %get-tuple-element.10), channel_id=1, source_target_pairs={{0,1},{1,2},{2,3},{3,4},{4,5},{5,6},{6,7},{7,8},{8,9},{9,10},{10,1... | collective-permute-start | bytes 36872 | tf_op jit(solution)/shard_map/ppermute | solution.py:358
  6.6 5.1 %collective-permute-start.1 = (f32[3,8,128]{2,1,0:T(8,128)S(1)}, f32[3,8,128]{2,1,0:T(8,128)S(1)}, u32[]{:S(2)}, u32[]{:S(2)}) collective-permute-start(f32[3,8,128]{2,1,0:T(8,128)S(1)} %get-tuple-element.11), channel_id=1, source_target_pairs={{0,15},{1,0},{2,1},{3,2},{4,3},{5,4},{6,5},{7,6},{8,7},{9,8},{10,9... | collective-permute-start | bytes 36872 | tf_op jit(solution)/shard_map/ppermute | solution.py:359
  12.6 11.1 %copy-start.4 = (f32[4,2]{0,1:T(2,128)S(1)}, f32[4,2]{0,1:T(2,128)}, u32[]{:S(2)}) copy-start(f32[4,2]{0,1:T(2,128)} %param.9) | copy-start | bytes 100
  12.6 30.3 %all-to-all-start = ((f32[32,40,128]{2,1,0:T(8,128)}), f32[32,40,128]{2,1,0:T(8,128)S(1)}, u32[]{:S(2)}, u32[]{:S(2)}) async-start(f32[32,40,128]{2,1,0:T(8,128)} %slots.1), calls=%async_computation | async-start | bytes 1310720 | tf_op jit(solution)/shard_map/all_to_all | solution.py:369

commit v2 on v1

--- a/solution.py
+++ b/solution.py
@@ -11,8 +11,8 @@
 SWAP = ("gy", "gx")
 CHUNK = 4
 WIDE = CHUNK + 2 * DEPTH
-SLOT = 40
-BACK = 16
+SLOT = 34
+BACK = 9
 UNROLL = (7, 4)
 GROUPS = (4, 4)
 PAD = 0
@@ -65,10 +65,19 @@
     )
 
 
-def turn_kernel(load_ref, mask_ref, gap_ref, ids_ref, rows_ref, first_ref, last_ref):
+def turn_kernel(*refs):
+    inputs, (rows_ref, first_ref, last_ref), scratch, sems = refs[:4], refs[4:7], refs[7:11], refs[11]
+    copies = [
+        pltpu.make_async_copy(source, target, sems.at[i])
+        for i, (source, target) in enumerate(zip(inputs, scratch))
+    ]
+    for copy in copies:
+        copy.start()
+    for copy in copies:
+        copy.wait()
+    load_ref, mask_ref, gap_ref, ids_ref = scratch
     flat = lambda v: v.reshape(64, 128)
-    low = jnp.where(mask_ref[...] > 0, -gap_ref[...], LOWEST)
-    low = flat(low)
+    low = flat(jnp.where(mask_ref[...] > 0, -gap_ref[...], LOWEST))
     ids = flat(ids_ref[...].astype(jnp.float32))
     pairs = (
         (flat(load_ref[0]), flat(load_ref[1])),
@@ -90,9 +99,10 @@
     lower = lax.broadcasted_iota(jnp.int32, (6, 128), 1) < 64
     for d in range(32):
         at = CHUNK * d + 8 - DEPTH
-        out_ref[d, 0:WIDE] = wide[0, at : at + WIDE]
-        out_ref[d, 16 : 16 + WIDE] = wide[1, at : at + WIDE]
-        out_ref[d, 32:38] = jnp.where(
+        to = SLOT * d
+        out_ref[to : to + WIDE] = wide[0, at : at + WIDE]
+        out_ref[to + WIDE : to + 2 * WIDE] = wide[1, at : at + WIDE]
+        out_ref[to + 2 * WIDE : to + SLOT] = jnp.where(
             lower, wide[2, at + 1 : at + 7], wide[2, at + 7 : at + 13]
         )
 
@@ -210,7 +220,7 @@
         p = PAD + k
         for v in range(2):
             b0, b1 = fetch(k, v)
-            b2, ids = fetch(16 + k, v)
+            b2, ids = fetch(WIDE + k, v)
             for c, b in enumerate((b0, b1, b2)):
                 b = step * b
                 u[c, p, v] = b
@@ -226,7 +236,7 @@
     loop(0, WIDE, unpack, UNROLL[0])
     for k in range(6):
         for v in range(2):
-            near, far = fetch(32 + k, v)
+            near, far = fetch(2 * WIDE + k, v)
             low[PAD + 1 + k, v] = near
             low[PAD + 7 + k, v] = far
 
@@ -324,11 +334,13 @@
 
 
 def bricks_kernel(in_ref, u_ref, w_ref, gaps_ref, rows):
-    top = jnp.max(in_ref[:, 8, :], axis=0, keepdims=True)
+    top = in_ref[pl.ds(2 * CHUNK, 32, stride=BACK), :]
+    top = jnp.max(top, axis=0, keepdims=True)
     gaps_ref[...] = jnp.broadcast_to(top[None], gaps_ref.shape)
     for d in range(32):
-        rows[0, CHUNK * d : CHUNK * d + CHUNK] = in_ref[d, 0:CHUNK]
-        rows[1, CHUNK * d : CHUNK * d + CHUNK] = in_ref[d, CHUNK : 2 * CHUNK]
+        for i in range(2):
+            at = BACK * d + CHUNK * i
+            rows[i, CHUNK * d : CHUNK * d + CHUNK] = in_ref[at : at + CHUNK]
     brick = u_ref.shape[1:]
     first = rows[0].T
     u_ref[0] = first[:64].reshape(brick)
@@ -340,33 +352,43 @@
     w_ref[2] = second[64:].reshape(brick)
 
 
+def swap(rows, each):
+    thin = 2 if each % 2 == 0 else 1
+    parts = rows.reshape(32, each // thin, thin, 128)
+    return lax.all_to_all(parts, SWAP, 0, 0, tiled=True).reshape(rows.shape)
+
+
 def shards(body_load, contact_mask, contact_gap, material_ids, lame_table):
     f32 = jnp.float32
     params = pltpu.CompilerParams(vmem_limit_bytes=32 * 1024 * 1024)
+    whole = pltpu.CompilerParams(vmem_limit_bytes=60 * 1024 * 1024)
     shape = lambda *dims: jax.ShapeDtypeStruct(dims, f32)
     vmem = pl.BlockSpec(memory_space=pltpu.VMEM)
     smem = pl.BlockSpec(memory_space=pltpu.SMEM)
+    inputs = (body_load, contact_mask, contact_gap, material_ids)
     rows, first, last = pl.pallas_call(
         turn_kernel,
         out_shape=(shape(3, 128, 128), shape(3, 8, 128), shape(3, 8, 128)),
-        in_specs=[vmem] * 4,
+        in_specs=[pl.BlockSpec(memory_space=pltpu.HBM)] * 4,
         out_specs=(vmem,) * 3,
-        compiler_params=params,
+        scratch_shapes=[pltpu.VMEM(a.shape, a.dtype) for a in inputs]
+        + [pltpu.SemaphoreType.DMA((4,))],
+        compiler_params=whole,
         name="turn",
-    )(body_load, contact_mask, contact_gap, material_ids)
+    )(*inputs)
     count = lax.axis_size("gz")
     before = lax.ppermute(last, "gz", [(i, (i + 1) % count) for i in range(count)])
     after = lax.ppermute(first, "gz", [(i, (i - 1) % count) for i in range(count)])
     slots = pl.pallas_call(
         slots_kernel,
-        out_shape=shape(32, SLOT, 128),
+        out_shape=shape(32 * SLOT, 128),
         in_specs=[vmem] * 3,
         out_specs=vmem,
         scratch_shapes=[pltpu.VMEM((3, 144, 128), f32)],
         compiler_params=params,
         name="slots",
     )(rows, before, after)
-    slots = lax.all_to_all(slots, SWAP, 0, 0, tiled=True)
+    slots = swap(slots, SLOT)
     gl, gm = bounds()
     back = pl.pallas_call(
         lambda *refs: iterate_kernel(gl, gm, *refs),
@@ -387,8 +409,8 @@
         ],
         compiler_params=params,
         name="iterate",
-    )(lame_table, slots.reshape(32 * SLOT, 128))
-    back = lax.all_to_all(back.reshape(32, BACK, 128), SWAP, 0, 0, tiled=True)
+    )(lame_table, slots)
+    back = swap(back, BACK)
     displacement, multiplier, gaps = pl.pallas_call(
         bricks_kernel,
         out_shape=(shape(*body_load.shape), shape(*body_load.shape), shape(count, 8, 128)),

time: 85.5 us -> 81.1 us (0.949)
  local copies, waits for them, and re-layouts: 3.25 us -> 1.02 us
  blocking collectives: 33.1 us -> 31.3 us
  waiting for transfers between devices: 19.9 us -> 18.3 us
  Pallas kernels: 9.53 us -> 10.9 us
    unnamed x11 -> x5, local copies, waits for them, and re-layouts: 3.25 us -> 1.02 us
    all_to_all x1, waiting for transfers between devices: 19.1 us -> 17.3 us  [swap(): return lax.all_to_all(parts, SWAP, 0, 0, tiled=True).reshape(rows.shape)]
    pallas_call x1, Pallas kernels: 0.13 us -> 1.74 us  [shards(): pl.pallas_call(turn_kernel, out_shape=(shape(3, 128, 128), shape(3, 8, 12...]
    all_to_all x1, blocking collectives: 15.6 us -> 14.3 us  [swap(): return lax.all_to_all(parts, SWAP, 0, 0, tiled=True).reshape(rows.shape)]
where the time goes in v2:
time: 81.1 us; the launch traced here: 80.8 us
  blocking collectives  31.3 us (39%)
  waiting for transfers between devices  18.3 us (23%)
  starting transfers between devices  18 us (22%)
  Pallas kernels  10.9 us (13%)
  local copies, waits for them, and re-layouts  1.02 us (1%)
    all_to_all x1, waiting for transfers between devices, swap(): return lax.all_to_all(parts, SWAP, 0, 0, tiled=True).reshape(rows.shape)  17.3 us
    all_to_all x1, blocking collectives, shards(): gaps = lax.all_to_all(gaps, 'gz', 0, 0, tiled=True)  16.9 us
    all_to_all x1, blocking collectives, swap(): return lax.all_to_all(parts, SWAP, 0, 0, tiled=True).reshape(rows.shape)  14.3 us
    all_to_all x1, starting transfers between devices, swap(): return lax.all_to_all(parts, SWAP, 0, 0, tiled=True).reshape(rows.shape)  11.1 us
    pallas_call x1, Pallas kernels, shards(): pl.pallas_call(lambda *refs: iterate_kernel(gl, gm, *refs), out_shape=sha...  7.53 us
    ppermute x1, starting transfers between devices, shards(): lax.ppermute(first, 'gz', [(i, (i - 1) % count) for i in range(count)])  4.22 us
    ppermute x1, starting transfers between devices, shards(): lax.ppermute(last, 'gz', [(i, (i + 1) % count) for i in range(count)])  2.7 us
    pallas_call x1, Pallas kernels, shards(): pl.pallas_call(turn_kernel, out_shape=(shape(3, 128, 128), shape(3, 8, 12...  1.74 us
  transfers between devices with their start and end apart: 3, of which 3 were waited for; matrix products, arithmetic and copies ran while one was open for 0% of the time, Pallas kernels for 0%

profile of v2, /device:TPU:1, one launch (start us, length us, event | category | flops | bytes accessed | tf_op | source)
XLA Modules:
  0.0 80.8 jit_solution(5111520819097487335)
XLA Ops:
  0.6 1.7 %turn.1 = (f32[3,128,128]{2,1,0:T(8,128)}, f32[3,8,128]{2,1,0:T(8,128)}, f32[3,8,128]{2,1,0:T(8,128)}) custom-call(f32[3,4,16,128]{3,2,1,0:T(8,128)} %refs_0_.2, s32[4,16,128]{2,1,0:T(8,128)} %refs_1_.1, f32[4,16,128]{2,1,0:T(8,128)} %refs_2_.1, s32[4,16,128]{2,1,0:T(8,128)} %refs_3_.1), custom_call_target="tpu_custom_call" | custom-call | tf_op jit(solution)/shard_map/turn/pallas_call | solution.py:369
  2.4 2.7 %collective-permute-start = (f32[3,8,128]{2,1,0:T(8,128)}, f32[3,8,128]{2,1,0:T(8,128)S(1)}, u32[]{:S(2)}, u32[]{:S(2)}) collective-permute-start(f32[3,8,128]{2,1,0:T(8,128)} %get-tuple-element.10), channel_id=1, source_target_pairs={{0,1},{1,2},{2,3},{3,4},{4,5},{5,6},{6,7},{7,8},{8,9},{9,10},{10,1... | collective-permute-start | bytes 36872 | tf_op jit(solution)/shard_map/ppermute | solution.py:380
  5.1 4.2 %collective-permute-start.1 = (f32[3,8,128]{2,1,0:T(8,128)}, f32[3,8,128]{2,1,0:T(8,128)S(1)}, u32[]{:S(2)}, u32[]{:S(2)}) collective-permute-start(f32[3,8,128]{2,1,0:T(8,128)} %get-tuple-element.11), channel_id=1, source_target_pairs={{0,15},{1,0},{2,1},{3,2},{4,3},{5,4},{6,5},{7,6},{8,7},{9,8},{10,9... | collective-permute-start | bytes 36872 | tf_op jit(solution)/shard_map/ppermute | solution.py:381
  9.3 0.9 %collective-permute-done.before_ref = f32[3,8,128]{2,1,0:T(8,128)S(1)} collective-permute-done((f32[3,8,128]{2,1,0:T(8,128)}, f32[3,8,128]{2,1,0:T(8,128)S(1)}, u32[]{:S(2)}, u32[]{:S(2)}) %collective-permute-start) | collective-permute-done | bytes 12320 | tf_op jit(solution)/shard_map/ppermute | solution.py:380
  10.2 0.2 collective-permute-done.1.after_ref
  10.3 0.0 copy-start
  10.3 0.9 %copy-done = f32[3,128,128]{2,1,0:T(8,128)S(1)} copy-done((f32[3,128,128]{2,1,0:T(8,128)S(1)}, f32[3,128,128]{2,1,0:T(8,128)}, u32[]{:S(2)}) %copy-start) | copy-done | bytes 196632
  11.3 0.9 %slots.1 = f32[1088,128]{1,0:T(8,128)} custom-call(f32[3,128,128]{2,1,0:T(8,128)S(1)} %copy-done, f32[3,8,128]{2,1,0:T(8,128)S(1)} %collective-permute-done.before_ref, f32[3,8,128]{2,1,0:T(8,128)S(1)} %collective-permute-done.1.after_ref), custom_call_target="tpu_custom_call" | custom-call | tf_op jit(solution)/shard_map/slots/pallas_call | solution.py:382
  12.1 0.0 copy-start.1
  12.1 11.1 %all-to-all-start = ((f32[32,17,2,128]{3,2,1,0:T(2,128)}), f32[32,17,2,128]{3,2,1,0:T(2,128)S(1)}, u32[]{:S(2)}, u32[]{:S(2)}) async-start(f32[32,17,2,128]{3,2,1,0:T(2,128)} %bitcast), calls=%async_computation | async-start | bytes 1114112 | tf_op jit(solution)/shard_map/all_to_all | solution.py:358
  23.2 0.0 copy-done.1
  23.2 0.1 copy.10.refs_0_
  23.3 17.3 %all-to-all-done = f32[32,17,2,128]{3,2,1,0:T(2,128)S(1)} async-done(((f32[32,17,2,128]{3,2,1,0:T(2,128)}), f32[32,17,2,128]{3,2,1,0:T(2,128)S(1)}, u32[]{:S(2)}, u32[]{:S(2)}) %all-to-all-start) | async-done | bytes 557088 | tf_op jit(solution)/shard_map/all_to_all | solution.py:358
  40.6 7.5 %iterate.1 = f32[288,128]{1,0:T(8,128)S(1)} custom-call(f32[4,2]{1,0:T(4,128)S(1)} %copy.10.refs_0_, f32[1088,128]{1,0:T(8,128)S(1)} %bitcast.4), custom_call_target="tpu_custom_call" | custom-call | tf_op jit(solution)/shard_map/iterate/pallas_call | solution.py:393
  48.1 14.3 %all_to_all.15 = f32[32,9,1,128]{3,2,1,0:T(1,128)S(1)} all-to-all(f32[32,9,1,128]{3,2,1,0:T(1,128)S(1)} %bitcast.6), channel_id=1, replica_groups=mesh['gx'=8,'gy'=4,'gz'=16] {'gy','gx'}, dimensions={0} | all-to-all | bytes 294912 | tf_op jit(solution)/shard_map/all_to_all | solution.py:358
  62.5 0.8 bricks.1
  63.3 16.9 %all_to_all.16 = f32[16,8,128]{2,1,0:T(8,128)S(1)} all-to-all(f32[16,8,128]{2,1,0:T(8,128)S(1)} %get-tuple-element.14), channel_id=1, replica_groups=mesh['gx'=8,'gy'=4,'gz'=16] {'gz'}, dimensions={0} | all-to-all | bytes 131072 | tf_op jit(solution)/shard_map/all_to_all | solution.py:423
  80.2 0.5 slice_reduce_fusion
Async XLA Ops:
  2.4 7.8 %collective-permute-start = (f32[3,8,128]{2,1,0:T(8,128)}, f32[3,8,128]{2,1,0:T(8,128)S(1)}, u32[]{:S(2)}, u32[]{:S(2)}) collective-permute-start(f32[3,8,128]{2,1,0:T(8,128)} %get-tuple-element.10), channel_id=1, source_target_pairs={{0,1},{1,2},{2,3},{3,4},{4,5},{5,6},{6,7},{7,8},{8,9},{9,10},{10,1... | collective-permute-start | bytes 36872 | tf_op jit(solution)/shard_map/ppermute | solution.py:380
  5.1 5.3 %collective-permute-start.1 = (f32[3,8,128]{2,1,0:T(8,128)}, f32[3,8,128]{2,1,0:T(8,128)S(1)}, u32[]{:S(2)}, u32[]{:S(2)}) collective-permute-start(f32[3,8,128]{2,1,0:T(8,128)} %get-tuple-element.11), channel_id=1, source_target_pairs={{0,15},{1,0},{2,1},{3,2},{4,3},{5,4},{6,5},{7,6},{8,7},{9,8},{10,9... | collective-permute-start | bytes 36872 | tf_op jit(solution)/shard_map/ppermute | solution.py:381
  10.3 0.9 %copy-start = (f32[3,128,128]{2,1,0:T(8,128)S(1)}, f32[3,128,128]{2,1,0:T(8,128)}, u32[]{:S(2)}) copy-start(f32[3,128,128]{2,1,0:T(8,128)} %get-tuple-element.9.rows_ref) | copy-start | bytes 589828
  12.1 11.1 %copy-start.1 = (f32[4,2]{0,1:T(2,128)S(1)}, f32[4,2]{0,1:T(2,128)}, u32[]{:S(2)}) copy-start(f32[4,2]{0,1:T(2,128)} %param.9) | copy-start | bytes 100
  12.1 28.5 %all-to-all-start = ((f32[32,17,2,128]{3,2,1,0:T(2,128)}), f32[32,17,2,128]{3,2,1,0:T(2,128)S(1)}, u32[]{:S(2)}, u32[]{:S(2)}) async-start(f32[32,17,2,128]{3,2,1,0:T(2,128)} %bitcast), calls=%async_computation | async-start | bytes 1114112 | tf_op jit(solution)/shard_map/all_to_all | solution.py:358

commit v3 on v2

--- a/solution.py
+++ b/solution.py
@@ -13,8 +13,9 @@
 WIDE = CHUNK + 2 * DEPTH
 SLOT = 34
 BACK = 9
-UNROLL = (7, 4)
-GROUPS = (4, 4)
+EDGE = 4
+UNROLL = (14, 13)
+GROUPS = (WIDE, WIDE - 2, WIDE, WIDE - 2)
 PAD = 0
 PLANES = WIDE + max(GROUPS)
 LOWEST = float(np.finfo(np.float32).min)
@@ -91,20 +92,36 @@
         last_ref[i] = turned[120:]
 
 
-def slots_kernel(rows_ref, before_ref, after_ref, out_ref, wide):
-    for i in range(3):
-        wide[i, 0:8] = before_ref[i]
-        wide[i, 8:136] = rows_ref[i]
-        wide[i, 136:144] = after_ref[i]
+def fill(out_ref, wide, first, begin, end, to):
     lower = lax.broadcasted_iota(jnp.int32, (6, 128), 1) < 64
-    for d in range(32):
-        at = CHUNK * d + 8 - DEPTH
-        to = SLOT * d
-        out_ref[to : to + WIDE] = wide[0, at : at + WIDE]
-        out_ref[to + WIDE : to + 2 * WIDE] = wide[1, at : at + WIDE]
-        out_ref[to + 2 * WIDE : to + SLOT] = jnp.where(
+    for d in range(begin, end):
+        at = CHUNK * d - DEPTH - first
+        row = SLOT * d - to
+        out_ref[row : row + WIDE] = wide[0, at : at + WIDE]
+        out_ref[row + WIDE : row + 2 * WIDE] = wide[1, at : at + WIDE]
+        out_ref[row + 2 * WIDE : row + SLOT] = jnp.where(
             lower, wide[2, at + 1 : at + 7], wide[2, at + 7 : at + 13]
         )
+
+
+def inner_kernel(rows_ref, out_ref):
+    fill(out_ref, rows_ref, 0, EDGE, 32 - EDGE, 0)
+
+
+def outer_kernel(rows_ref, before_ref, after_ref, _, out_ref, wide, part, sems):
+    for i in range(3):
+        wide[0, i, 0:8] = before_ref[i]
+        wide[0, i, 8:32] = rows_ref[i, 0:24]
+        wide[1, i, 0:24] = rows_ref[i, 104:128]
+        wide[1, i, 24:32] = after_ref[i]
+    copies = []
+    for side, begin, first in ((0, 0, -8), (1, 32 - EDGE, 104)):
+        fill(part.at[side], wide.at[side], first, begin, begin + EDGE, SLOT * begin)
+        target = out_ref.at[pl.ds(SLOT * begin, SLOT * EDGE)]
+        copies.append(pltpu.make_async_copy(part.at[side], target, sems.at[side]))
+        copies[-1].start()
+    for copy in copies:
+        copy.wait()
 
 
 def flip(v, even):
@@ -189,6 +206,8 @@
 
 
 def planes(lo, hi, group, body):
+    group = min(group, hi - lo)
+
     def step(g, _):
         for j in range(group):
             body(lo + g * group + j)
@@ -196,7 +215,7 @@
     lax.fori_loop(0, -(-(hi - lo) // group), step, None)
 
 
-def iterate_kernel(gl, gm, table_ref, in_ref, out_ref, u, u1, quad, dual, dist, low, lam, mu, modes, forces):
+def iterate_kernel(gl, gm, table_ref, in_ref, out_ref, u, u1, quad, dual, dist, low, lam, mu, halfway, modes, forces):
     lane = lax.broadcasted_iota(jnp.int32, (8, 128), 1)
     left = lane < 64
     x_up, x_down, y_up, y_down = make_shifts()
@@ -268,10 +287,15 @@
         other = shift(value)
         return (add(other, value), sub(other, value))
 
-    def forward(p):
+    def forward_y(p):
         for c in range(3):
             for m, part in enumerate(split(pair(u, c, p), y_up)):
-                for k, value in enumerate(split(part, x_up)):
+                put(halfway, part, c, m, p)
+
+    def forward_x(p):
+        for c in range(3):
+            for m in range(2):
+                for k, value in enumerate(split(pair(halfway, c, m, p), x_up)):
                     put(modes, value, c, 2 * m + k, p)
 
     def layer(v):
@@ -292,10 +316,16 @@
     def merge(s, d, shift):
         return add(sub(s, d), shift(add(s, d)))
 
-    def backward(p):
+    def backward_x(p):
         for c in range(3):
             f = [pair(forces, c, m, p) for m in range(4)]
-            total = merge(merge(f[0], f[1], x_down), merge(f[2], f[3], x_down), y_down)
+            ys, yd = merge(f[0], f[1], x_down), merge(f[2], f[3], x_down)
+            put(halfway, sub(ys, yd), c, 0, p)
+            put(halfway, add(ys, yd), c, 1, p)
+
+    def backward_y(p):
+        for c in range(3):
+            total = add(pair(halfway, c, 0, p), y_down(pair(halfway, c, 1, p)))
             new = add(sub(pair(u, c, p), total), pair(u1, c, p))
             if c == 2:
                 new = sub(new, pair(quad, p))
@@ -308,12 +338,14 @@
     zero = jnp.zeros((8, 128), jnp.float32)
     for t in range(1, ITERS):
         lo, hi = PAD + t, PAD + WIDE - 1 - t
-        planes(lo - 1, hi + 2, GROUPS[0], forward)
+        planes(lo - 1, hi + 2, GROUPS[0], forward_y)
+        planes(lo - 1, hi + 2, GROUPS[2], forward_x)
         for v in range(2):
             below = [[modes[c, m, lo - 1, v] for m in range(4)] for c in range(3)]
             held = [[zero] * 4 for _ in range(3)]
-            lax.fori_loop(lo - 1, hi + 1, layer(v), (held, below), unroll=UNROLL[1])
-        planes(lo, hi + 1, GROUPS[1], backward)
+            lax.fori_loop(lo - 1, hi + 1, layer(v), (held, below), unroll=min(UNROLL[1], hi + 2 - lo))
+        planes(lo, hi + 1, GROUPS[1], backward_x)
+        planes(lo, hi + 1, GROUPS[3], backward_y)
         history.append(largest())
     gaps = jnp.zeros((8, 128), jnp.float32)
     for t, top in enumerate(history):
@@ -333,10 +365,13 @@
         out_ref[pl.ds(i * BACK + 8, 8, stride=4 * BACK), :] = gaps
 
 
-def bricks_kernel(in_ref, u_ref, w_ref, gaps_ref, rows):
+def gaps_kernel(in_ref, gaps_ref):
     top = in_ref[pl.ds(2 * CHUNK, 32, stride=BACK), :]
     top = jnp.max(top, axis=0, keepdims=True)
     gaps_ref[...] = jnp.broadcast_to(top[None], gaps_ref.shape)
+
+
+def bricks_kernel(in_ref, u_ref, w_ref, rows):
     for d in range(32):
         for i in range(2):
             at = BACK * d + CHUNK * i
@@ -365,11 +400,12 @@
     shape = lambda *dims: jax.ShapeDtypeStruct(dims, f32)
     vmem = pl.BlockSpec(memory_space=pltpu.VMEM)
     smem = pl.BlockSpec(memory_space=pltpu.SMEM)
+    hbm = pl.BlockSpec(memory_space=pltpu.HBM)
     inputs = (body_load, contact_mask, contact_gap, material_ids)
     rows, first, last = pl.pallas_call(
         turn_kernel,
         out_shape=(shape(3, 128, 128), shape(3, 8, 128), shape(3, 8, 128)),
-        in_specs=[pl.BlockSpec(memory_space=pltpu.HBM)] * 4,
+        in_specs=[hbm] * 4,
         out_specs=(vmem,) * 3,
         scratch_shapes=[pltpu.VMEM(a.shape, a.dtype) for a in inputs]
         + [pltpu.SemaphoreType.DMA((4,))],
@@ -380,14 +416,28 @@
     before = lax.ppermute(last, "gz", [(i, (i + 1) % count) for i in range(count)])
     after = lax.ppermute(first, "gz", [(i, (i - 1) % count) for i in range(count)])
     slots = pl.pallas_call(
-        slots_kernel,
+        inner_kernel,
         out_shape=shape(32 * SLOT, 128),
-        in_specs=[vmem] * 3,
+        in_specs=[vmem],
         out_specs=vmem,
-        scratch_shapes=[pltpu.VMEM((3, 144, 128), f32)],
         compiler_params=params,
-        name="slots",
-    )(rows, before, after)
+        cost_estimate=pl.CostEstimate(flops=0, bytes_accessed=1 << 22, transcendentals=0),
+        name="inner",
+    )(rows)
+    slots = pl.pallas_call(
+        outer_kernel,
+        out_shape=shape(32 * SLOT, 128),
+        in_specs=[vmem] * 3 + [hbm],
+        out_specs=hbm,
+        scratch_shapes=[
+            pltpu.VMEM((2, 3, 32, 128), f32),
+            pltpu.VMEM((2, SLOT * EDGE, 128), f32),
+            pltpu.SemaphoreType.DMA((2,)),
+        ],
+        input_output_aliases={3: 0},
+        compiler_params=params,
+        name="outer",
+    )(rows, before, after, slots)
     slots = swap(slots, SLOT)
     gl, gm = bounds()
     back = pl.pallas_call(
@@ -404,6 +454,7 @@
             pltpu.VMEM((PLANES, 2, 8, 128), f32),
             pltpu.VMEM((PLANES, 2, 8, 128), f32),
             pltpu.VMEM((PLANES, 2, 8, 128), f32),
+            pltpu.VMEM((3, 2, PLANES, 2, 8, 128), f32),
             pltpu.VMEM((3, 4, PLANES, 2, 8, 128), f32),
             pltpu.VMEM((3, 4, PLANES, 2, 8, 128), f32),
         ],
@@ -411,13 +462,22 @@
         name="iterate",
     )(lame_table, slots)
     back = swap(back, BACK)
-    displacement, multiplier, gaps = pl.pallas_call(
+    gaps = pl.pallas_call(
+        gaps_kernel,
+        out_shape=shape(count, 1, 128),
+        in_specs=[vmem],
+        out_specs=vmem,
+        compiler_params=params,
+        name="gaps",
+    )(back)
+    displacement, multiplier = pl.pallas_call(
         bricks_kernel,
-        out_shape=(shape(*body_load.shape), shape(*body_load.shape), shape(count, 8, 128)),
+        out_shape=(shape(*body_load.shape), shape(*body_load.shape)),
         in_specs=[vmem],
-        out_specs=(vmem,) * 3,
+        out_specs=(vmem,) * 2,
         scratch_shapes=[pltpu.VMEM((2, 128, 128), f32)],
         compiler_params=params,
+        cost_estimate=pl.CostEstimate(flops=0, bytes_accessed=1 << 22, transcendentals=0),
         name="bricks",
     )(back)
     gaps = lax.all_to_all(gaps, "gz", 0, 0, tiled=True)

time: 81.1 us -> 76.2 us (0.940)
  blocking collectives: 31.3 us -> 14.5 us
  starting transfers between devices: 18 us -> 26.6 us
  waiting for transfers between devices: 18.3 us -> 23.4 us
  Pallas kernels: 10.9 us -> 9.2 us
    all_to_all x1 -> x0, blocking collectives: 16.9 us -> none  [shards(): gaps = lax.all_to_all(gaps, 'gz', 0, 0, tiled=True)]
    all_to_all x0 -> x1, starting transfers between devices: none -> 9.43 us  [shards(): gaps = lax.all_to_all(gaps, 'gz', 0, 0, tiled=True)]
    all_to_all x0 -> x1, waiting for transfers between devices: none -> 6.23 us  [shards(): gaps = lax.all_to_all(gaps, 'gz', 0, 0, tiled=True)]
    pallas_call x1, Pallas kernels: 7.53 us -> 4.53 us  [shards(): pl.pallas_call(lambda *refs: iterate_kernel(gl, gm, *refs), out_shape=sha...]
    pallas_call x1 -> x3, Pallas kernels: 0.87 us -> 2.15 us  [the longest x1 0.85 us: shards(): pl.pallas_call(inner_kernel, out_shape=shape(32 * SLOT, 128), in_specs=[v...]
    ppermute x1, waiting for transfers between devices: 0.86 us -> 0.01 us  [shards(): lax.ppermute(last, 'gz', [(i, (i + 1) % count) for i in range(count)])]
    all_to_all x1, starting transfers between devices: 11.1 us -> 10.2 us  [swap(): return lax.all_to_all(parts, SWAP, 0, 0, tiled=True).reshape(rows.shape)]
  transfers between devices with their start and end apart: 3 -> 4, of which waited for: 3 -> 2; matrix products, arithmetic and copies ran while one was open for 0% -> 0% of each run, Pallas kernels for 0% -> 2%
where the time goes in v3:
time: 76.2 us; the launch traced here: 75.9 us
  starting transfers between devices  26.6 us (35%)
  waiting for transfers between devices  23.4 us (31%)
  blocking collectives  14.5 us (19%)
  Pallas kernels  9.2 us (12%)
  local copies, waits for them, and re-layouts  1.03 us (1%)
    all_to_all x1, waiting for transfers between devices, swap(): return lax.all_to_all(parts, SWAP, 0, 0, tiled=True).reshape(rows.shape)  17.1 us
    all_to_all x1, blocking collectives, swap(): return lax.all_to_all(parts, SWAP, 0, 0, tiled=True).reshape(rows.shape)  14.5 us
    all_to_all x1, starting transfers between devices, swap(): return lax.all_to_all(parts, SWAP, 0, 0, tiled=True).reshape(rows.shape)  10.2 us
    all_to_all x1, starting transfers between devices, shards(): gaps = lax.all_to_all(gaps, 'gz', 0, 0, tiled=True)  9.43 us
    all_to_all x1, waiting for transfers between devices, shards(): gaps = lax.all_to_all(gaps, 'gz', 0, 0, tiled=True)  6.23 us
    pallas_call x1, Pallas kernels, shards(): pl.pallas_call(lambda *refs: iterate_kernel(gl, gm, *refs), out_shape=sha...  4.53 us
    ppermute x1, starting transfers between devices, shards(): lax.ppermute(first, 'gz', [(i, (i - 1) % count) for i in range(count)])  4.22 us
    ppermute x1, starting transfers between devices, shards(): lax.ppermute(last, 'gz', [(i, (i + 1) % count) for i in range(count)])  2.7 us
  transfers between devices with their start and end apart: 4, of which 2 were waited for; matrix products, arithmetic and copies ran while one was open for 0% of the time, Pallas kernels for 2%

profile of v3, /device:TPU:1, one launch (start us, length us, event | category | flops | bytes accessed | tf_op | source)
XLA Modules:
  0.0 75.9 jit_solution(2865290426315380899)
XLA Ops:
  0.6 1.7 %turn.1 = (f32[3,128,128]{2,1,0:T(8,128)}, f32[3,8,128]{2,1,0:T(8,128)}, f32[3,8,128]{2,1,0:T(8,128)}) custom-call(f32[3,4,16,128]{3,2,1,0:T(8,128)} %refs_0_.2, s32[4,16,128]{2,1,0:T(8,128)} %refs_1_.1, f32[4,16,128]{2,1,0:T(8,128)} %refs_2_.1, s32[4,16,128]{2,1,0:T(8,128)} %refs_3_.1), custom_call_target="tpu_custom_call" | custom-call | tf_op jit(solution)/shard_map/turn/pallas_call | solution.py:405
  2.4 2.7 %collective-permute-start = (f32[3,8,128]{2,1,0:T(8,128)}, f32[3,8,128]{2,1,0:T(8,128)S(1)}, u32[]{:S(2)}, u32[]{:S(2)}) collective-permute-start(f32[3,8,128]{2,1,0:T(8,128)} %get-tuple-element.9), channel_id=1, source_target_pairs={{0,1},{1,2},{2,3},{3,4},{4,5},{5,6},{6,7},{7,8},{8,9},{9,10},{10,1... | collective-permute-start | bytes 36872 | tf_op jit(solution)/shard_map/ppermute | solution.py:416
  5.1 4.2 %collective-permute-start.1 = (f32[3,8,128]{2,1,0:T(8,128)}, f32[3,8,128]{2,1,0:T(8,128)S(1)}, u32[]{:S(2)}, u32[]{:S(2)}) collective-permute-start(f32[3,8,128]{2,1,0:T(8,128)} %get-tuple-element.10), channel_id=1, source_target_pairs={{0,15},{1,0},{2,1},{3,2},{4,3},{5,4},{6,5},{7,6},{8,7},{9,8},{10,9... | collective-permute-start | bytes 36872 | tf_op jit(solution)/shard_map/ppermute | solution.py:417
  9.3 0.0 copy-start
  9.3 0.9 %copy-done = f32[3,128,128]{2,1,0:T(8,128)S(1)} copy-done((f32[3,128,128]{2,1,0:T(8,128)S(1)}, f32[3,128,128]{2,1,0:T(8,128)}, u32[]{:S(2)}) %copy-start) | copy-done | bytes 196632
  10.2 0.8 %inner.1._ = f32[1088,128]{1,0:T(8,128)} custom-call(f32[3,128,128]{2,1,0:T(8,128)S(1)} %copy-done), custom_call_target="tpu_custom_call" | custom-call | bytes 4194304 | tf_op jit(solution)/shard_map/inner/pallas_call | solution.py:418
  11.1 0.0 collective-permute-done.before_ref
  11.1 0.0 collective-permute-done.1.after_ref
  11.1 0.7 outer.1
  11.8 0.0 copy-start.1
  11.8 10.2 %all-to-all-start = ((f32[32,17,2,128]{3,2,1,0:T(2,128)}), f32[32,17,2,128]{3,2,1,0:T(2,128)S(1)}, u32[]{:S(2)}, u32[]{:S(2)}) async-start(f32[32,17,2,128]{3,2,1,0:T(2,128)} %bitcast), calls=%async_computation | async-start | bytes 1114112 | tf_op jit(solution)/shard_map/all_to_all | solution.py:393
  22.0 0.0 copy-done.1
  22.0 0.1 copy.11.refs_0_
  22.1 17.1 %all-to-all-done = f32[32,17,2,128]{3,2,1,0:T(2,128)S(1)} async-done(((f32[32,17,2,128]{3,2,1,0:T(2,128)}), f32[32,17,2,128]{3,2,1,0:T(2,128)S(1)}, u32[]{:S(2)}, u32[]{:S(2)}) %all-to-all-start) | async-done | bytes 557088 | tf_op jit(solution)/shard_map/all_to_all | solution.py:393
  39.2 4.5 %iterate.1 = f32[288,128]{1,0:T(8,128)S(1)} custom-call(f32[4,2]{1,0:T(4,128)S(1)} %copy.11.refs_0_, f32[1088,128]{1,0:T(8,128)S(1)} %bitcast.4), custom_call_target="tpu_custom_call" | custom-call | tf_op jit(solution)/shard_map/iterate/pallas_call | solution.py:443
  43.8 14.5 %all_to_all.15 = f32[32,9,1,128]{3,2,1,0:T(1,128)S(1)} all-to-all(f32[32,9,1,128]{3,2,1,0:T(1,128)S(1)} %bitcast.7), channel_id=1, replica_groups=mesh['gx'=8,'gy'=4,'gz'=16] {'gy','gx'}, dimensions={0} | all-to-all | bytes 294912 | tf_op jit(solution)/shard_map/all_to_all | solution.py:393
  58.3 0.6 gaps.1
  58.9 9.4 %all-to-all-start.2 = ((f32[16,1,128]{2,1,0:T(1,128)}), f32[16,1,128]{2,1,0:T(1,128)S(1)}, u32[]{:S(2)}, u32[]{:S(2)}) async-start(f32[16,1,128]{2,1,0:T(1,128)} %gaps.1), calls=%async_computation.2 | async-start | bytes 16384 | tf_op jit(solution)/shard_map/all_to_all | solution.py:483
  68.3 0.8 %bricks.1 = (f32[3,4,16,128]{3,2,1,0:T(8,128)}, f32[3,4,16,128]{3,2,1,0:T(8,128)}) custom-call(f32[288,128]{1,0:T(8,128)S(1)} %bitcast.6), custom_call_target="tpu_custom_call" | custom-call | bytes 4194304 | tf_op jit(solution)/shard_map/bricks/pallas_call | solution.py:473
  69.1 6.2 %all-to-all-done.2 = f32[16,1,128]{2,1,0:T(1,128)S(1)} async-done(((f32[16,1,128]{2,1,0:T(1,128)}), f32[16,1,128]{2,1,0:T(1,128)S(1)}, u32[]{:S(2)}, u32[]{:S(2)}) %all-to-all-start.2) | async-done | bytes 8224 | tf_op jit(solution)/shard_map/all_to_all | solution.py:483
  75.3 0.5 slice_reduce_fusion
Async XLA Ops:
  2.4 8.7 %collective-permute-start = (f32[3,8,128]{2,1,0:T(8,128)}, f32[3,8,128]{2,1,0:T(8,128)S(1)}, u32[]{:S(2)}, u32[]{:S(2)}) collective-permute-start(f32[3,8,128]{2,1,0:T(8,128)} %get-tuple-element.9), channel_id=1, source_target_pairs={{0,1},{1,2},{2,3},{3,4},{4,5},{5,6},{6,7},{7,8},{8,9},{9,10},{10,1... | collective-permute-start | bytes 36872 | tf_op jit(solution)/shard_map/ppermute | solution.py:416
  5.1 6.0 %collective-permute-start.1 = (f32[3,8,128]{2,1,0:T(8,128)}, f32[3,8,128]{2,1,0:T(8,128)S(1)}, u32[]{:S(2)}, u32[]{:S(2)}) collective-permute-start(f32[3,8,128]{2,1,0:T(8,128)} %get-tuple-element.10), channel_id=1, source_target_pairs={{0,15},{1,0},{2,1},{3,2},{4,3},{5,4},{6,5},{7,6},{8,7},{9,8},{10,9... | collective-permute-start | bytes 36872 | tf_op jit(solution)/shard_map/ppermute | solution.py:417
  9.3 0.9 %copy-start = (f32[3,128,128]{2,1,0:T(8,128)S(1)}, f32[3,128,128]{2,1,0:T(8,128)}, u32[]{:S(2)}) copy-start(f32[3,128,128]{2,1,0:T(8,128)} %get-tuple-element.8.rows_ref) | copy-start | bytes 589828
  11.8 10.3 %copy-start.1 = (f32[4,2]{0,1:T(2,128)S(1)}, f32[4,2]{0,1:T(2,128)}, u32[]{:S(2)}) copy-start(f32[4,2]{0,1:T(2,128)} %param.9) | copy-start | bytes 100
  11.8 27.5 %all-to-all-start = ((f32[32,17,2,128]{3,2,1,0:T(2,128)}), f32[32,17,2,128]{3,2,1,0:T(2,128)S(1)}, u32[]{:S(2)}, u32[]{:S(2)}) async-start(f32[32,17,2,128]{3,2,1,0:T(2,128)} %bitcast), calls=%async_computation | async-start | bytes 1114112 | tf_op jit(solution)/shard_map/all_to_all | solution.py:393
  58.9 16.4 %all-to-all-start.2 = ((f32[16,1,128]{2,1,0:T(1,128)}), f32[16,1,128]{2,1,0:T(1,128)S(1)}, u32[]{:S(2)}, u32[]{:S(2)}) async-start(f32[16,1,128]{2,1,0:T(1,128)} %gaps.1), calls=%async_computation.2 | async-start | bytes 16384 | tf_op jit(solution)/shard_map/all_to_all | solution.py:483

commit v4 on v3

--- a/solution.py
+++ b/solution.py
@@ -67,16 +67,15 @@
 
 
 def turn_kernel(*refs):
-    inputs, (rows_ref, first_ref, last_ref), scratch, sems = refs[:4], refs[4:7], refs[7:11], refs[11]
-    copies = [
-        pltpu.make_async_copy(source, target, sems.at[i])
-        for i, (source, target) in enumerate(zip(inputs, scratch))
-    ]
-    for copy in copies:
+    load, mask, gap, ids, rows_ref, first_ref, last_ref = refs[:7]
+    load_ref, mask_ref, gap_ref, ids_ref, turned, in_sems, out_sems = refs[7:]
+    pieces = [(load.at[i], load_ref.at[i]) for i in range(3)]
+    pieces += [(mask, mask_ref), (gap, gap_ref), (ids, ids_ref)]
+    incoming = [pltpu.make_async_copy(*piece, in_sems.at[i]) for i, piece in enumerate(pieces)]
+    for copy in incoming:
         copy.start()
-    for copy in copies:
+    for copy in incoming:
         copy.wait()
-    load_ref, mask_ref, gap_ref, ids_ref = scratch
     flat = lambda v: v.reshape(64, 128)
     low = flat(jnp.where(mask_ref[...] > 0, -gap_ref[...], LOWEST))
     ids = flat(ids_ref[...].astype(jnp.float32))
@@ -85,11 +84,20 @@
         (flat(load_ref[2]), ids),
         (low, low),
     )
+    outgoing = []
     for i, pair in enumerate(pairs):
-        turned = jnp.concatenate(pair, 0).T
-        rows_ref[i] = turned
-        first_ref[i] = turned[:8]
-        last_ref[i] = turned[120:]
+        turned[i] = jnp.concatenate(pair, 0).T
+        for k, (source, target) in enumerate(
+            (
+                (turned.at[i], rows_ref.at[i]),
+                (turned.at[i, pl.ds(0, 8)], first_ref.at[i]),
+                (turned.at[i, pl.ds(120, 8)], last_ref.at[i]),
+            )
+        ):
+            outgoing.append(pltpu.make_async_copy(source, target, out_sems.at[i, k]))
+            outgoing[-1].start()
+    for copy in outgoing:
+        copy.wait()
 
 
 def fill(out_ref, wide, first, begin, end, to):
@@ -104,8 +112,16 @@
         )
 
 
-def inner_kernel(rows_ref, out_ref):
-    fill(out_ref, rows_ref, 0, EDGE, 32 - EDGE, 0)
+def inner_kernel(rows_ref, out_ref, part, sems):
+    copies = []
+    for side in range(32 // EDGE - 2):
+        begin = EDGE * (side + 1)
+        fill(part.at[side], rows_ref, 0, begin, begin + EDGE, SLOT * begin)
+        target = out_ref.at[pl.ds(SLOT * begin, SLOT * EDGE)]
+        copies.append(pltpu.make_async_copy(part.at[side], target, sems.at[side]))
+        copies[-1].start()
+    for copy in copies:
+        copy.wait()
 
 
 def outer_kernel(rows_ref, before_ref, after_ref, _, out_ref, wide, part, sems):
@@ -406,9 +422,13 @@
         turn_kernel,
         out_shape=(shape(3, 128, 128), shape(3, 8, 128), shape(3, 8, 128)),
         in_specs=[hbm] * 4,
-        out_specs=(vmem,) * 3,
+        out_specs=(hbm,) * 3,
         scratch_shapes=[pltpu.VMEM(a.shape, a.dtype) for a in inputs]
-        + [pltpu.SemaphoreType.DMA((4,))],
+        + [
+            pltpu.VMEM((3, 128, 128), f32),
+            pltpu.SemaphoreType.DMA((6,)),
+            pltpu.SemaphoreType.DMA((3, 3)),
+        ],
         compiler_params=whole,
         name="turn",
     )(*inputs)
@@ -419,7 +439,11 @@
         inner_kernel,
         out_shape=shape(32 * SLOT, 128),
         in_specs=[vmem],
-        out_specs=vmem,
+        out_specs=hbm,
+        scratch_shapes=[
+            pltpu.VMEM((32 // EDGE - 2, SLOT * EDGE, 128), f32),
+            pltpu.SemaphoreType.DMA((32 // EDGE - 2,)),
+        ],
         compiler_params=params,
         cost_estimate=pl.CostEstimate(flops=0, bytes_accessed=1 << 22, transcendentals=0),
         name="inner",

time: 76.2 us -> 76.2 us (level)
  no operation moved by 1% of the time
where the time goes in v4:
time: 76.2 us; the launch traced here: 75.9 us
  starting transfers between devices  26.6 us (35%)
  waiting for transfers between devices  23.4 us (31%)
  blocking collectives  14.5 us (19%)
  Pallas kernels  9.17 us (12%)
  local copies, waits for them, and re-layouts  1.03 us (1%)
    all_to_all x1, waiting for transfers between devices, swap(): return lax.all_to_all(parts, SWAP, 0, 0, tiled=True).reshape(rows.shape)  17.1 us
    all_to_all x1, blocking collectives, swap(): return lax.all_to_all(parts, SWAP, 0, 0, tiled=True).reshape(rows.shape)  14.5 us
    all_to_all x1, starting transfers between devices, swap(): return lax.all_to_all(parts, SWAP, 0, 0, tiled=True).reshape(rows.shape)  10.2 us
    all_to_all x1, starting transfers between devices, shards(): gaps = lax.all_to_all(gaps, 'gz', 0, 0, tiled=True)  9.41 us
    all_to_all x1, waiting for transfers between devices, shards(): gaps = lax.all_to_all(gaps, 'gz', 0, 0, tiled=True)  6.23 us
    pallas_call x1, Pallas kernels, shards(): pl.pallas_call(lambda *refs: iterate_kernel(gl, gm, *refs), out_shape=sha...  4.53 us
    ppermute x1, starting transfers between devices, shards(): lax.ppermute(first, 'gz', [(i, (i - 1) % count) for i in range(count)])  4.22 us
    ppermute x1, starting transfers between devices, shards(): lax.ppermute(last, 'gz', [(i, (i + 1) % count) for i in range(count)])  2.7 us
  transfers between devices with their start and end apart: 4, of which 2 were waited for; matrix products, arithmetic and copies ran while one was open for 0% of the time, Pallas kernels for 2%

profile of v4, /device:TPU:1, one launch (start us, length us, event | category | flops | bytes accessed | tf_op | source)
XLA Modules:
  0.0 75.9 jit_solution(10059464079105002412)
XLA Ops:
  0.6 1.7 %turn.1 = (f32[3,128,128]{2,1,0:T(8,128)}, f32[3,8,128]{2,1,0:T(8,128)}, f32[3,8,128]{2,1,0:T(8,128)}) custom-call(f32[3,4,16,128]{3,2,1,0:T(8,128)} %refs_0_.2, s32[4,16,128]{2,1,0:T(8,128)} %refs_1_.1, f32[4,16,128]{2,1,0:T(8,128)} %refs_2_.1, s32[4,16,128]{2,1,0:T(8,128)} %refs_3_.1), custom_call_target="tpu_custom_call" | custom-call | tf_op jit(solution)/shard_map/turn/pallas_call | solution.py:421
  2.4 2.7 %collective-permute-start = (f32[3,8,128]{2,1,0:T(8,128)}, f32[3,8,128]{2,1,0:T(8,128)S(1)}, u32[]{:S(2)}, u32[]{:S(2)}) collective-permute-start(f32[3,8,128]{2,1,0:T(8,128)} %get-tuple-element.9), channel_id=1, source_target_pairs={{0,1},{1,2},{2,3},{3,4},{4,5},{5,6},{6,7},{7,8},{8,9},{9,10},{10,1... | collective-permute-start | bytes 36872 | tf_op jit(solution)/shard_map/ppermute | solution.py:436
  5.1 4.2 %collective-permute-start.1 = (f32[3,8,128]{2,1,0:T(8,128)}, f32[3,8,128]{2,1,0:T(8,128)S(1)}, u32[]{:S(2)}, u32[]{:S(2)}) collective-permute-start(f32[3,8,128]{2,1,0:T(8,128)} %get-tuple-element.10), channel_id=1, source_target_pairs={{0,15},{1,0},{2,1},{3,2},{4,3},{5,4},{6,5},{7,6},{8,7},{9,8},{10,9... | collective-permute-start | bytes 36872 | tf_op jit(solution)/shard_map/ppermute | solution.py:437
  9.3 0.0 copy-start
  9.3 0.9 %copy-done = f32[3,128,128]{2,1,0:T(8,128)S(1)} copy-done((f32[3,128,128]{2,1,0:T(8,128)S(1)}, f32[3,128,128]{2,1,0:T(8,128)}, u32[]{:S(2)}) %copy-start) | copy-done | bytes 196632
  10.2 0.8 %inner.1._ = f32[1088,128]{1,0:T(8,128)} custom-call(f32[3,128,128]{2,1,0:T(8,128)S(1)} %copy-done), custom_call_target="tpu_custom_call" | custom-call | bytes 4194304 | tf_op jit(solution)/shard_map/inner/pallas_call | solution.py:438
  11.0 0.0 collective-permute-done.before_ref
  11.1 0.0 collective-permute-done.1.after_ref
  11.1 0.7 outer.1
  11.8 0.0 copy-start.1
  11.8 10.2 %all-to-all-start = ((f32[32,17,2,128]{3,2,1,0:T(2,128)}), f32[32,17,2,128]{3,2,1,0:T(2,128)S(1)}, u32[]{:S(2)}, u32[]{:S(2)}) async-start(f32[32,17,2,128]{3,2,1,0:T(2,128)} %bitcast), calls=%async_computation | async-start | bytes 1114112 | tf_op jit(solution)/shard_map/all_to_all | solution.py:409
  22.0 0.0 copy-done.1
  22.0 0.1 copy.11.refs_0_
  22.1 17.1 %all-to-all-done = f32[32,17,2,128]{3,2,1,0:T(2,128)S(1)} async-done(((f32[32,17,2,128]{3,2,1,0:T(2,128)}), f32[32,17,2,128]{3,2,1,0:T(2,128)S(1)}, u32[]{:S(2)}, u32[]{:S(2)}) %all-to-all-start) | async-done | bytes 557088 | tf_op jit(solution)/shard_map/all_to_all | solution.py:409
  39.3 4.5 %iterate.1 = f32[288,128]{1,0:T(8,128)S(1)} custom-call(f32[4,2]{1,0:T(4,128)S(1)} %copy.11.refs_0_, f32[1088,128]{1,0:T(8,128)S(1)} %bitcast.4), custom_call_target="tpu_custom_call" | custom-call | tf_op jit(solution)/shard_map/iterate/pallas_call | solution.py:467
  43.8 14.5 %all_to_all.15 = f32[32,9,1,128]{3,2,1,0:T(1,128)S(1)} all-to-all(f32[32,9,1,128]{3,2,1,0:T(1,128)S(1)} %bitcast.7), channel_id=1, replica_groups=mesh['gx'=8,'gy'=4,'gz'=16] {'gy','gx'}, dimensions={0} | all-to-all | bytes 294912 | tf_op jit(solution)/shard_map/all_to_all | solution.py:409
  58.3 0.6 gaps.1
  58.9 9.4 %all-to-all-start.2 = ((f32[16,1,128]{2,1,0:T(1,128)}), f32[16,1,128]{2,1,0:T(1,128)S(1)}, u32[]{:S(2)}, u32[]{:S(2)}) async-start(f32[16,1,128]{2,1,0:T(1,128)} %gaps.1), calls=%async_computation.2 | async-start | bytes 16384 | tf_op jit(solution)/shard_map/all_to_all | solution.py:507
  68.3 0.8 %bricks.1 = (f32[3,4,16,128]{3,2,1,0:T(8,128)}, f32[3,4,16,128]{3,2,1,0:T(8,128)}) custom-call(f32[288,128]{1,0:T(8,128)S(1)} %bitcast.6), custom_call_target="tpu_custom_call" | custom-call | bytes 4194304 | tf_op jit(solution)/shard_map/bricks/pallas_call | solution.py:497
  69.1 6.2 %all-to-all-done.2 = f32[16,1,128]{2,1,0:T(1,128)S(1)} async-done(((f32[16,1,128]{2,1,0:T(1,128)}), f32[16,1,128]{2,1,0:T(1,128)S(1)}, u32[]{:S(2)}, u32[]{:S(2)}) %all-to-all-start.2) | async-done | bytes 8224 | tf_op jit(solution)/shard_map/all_to_all | solution.py:507
  75.3 0.5 slice_reduce_fusion
Async XLA Ops:
  2.4 8.7 %collective-permute-start = (f32[3,8,128]{2,1,0:T(8,128)}, f32[3,8,128]{2,1,0:T(8,128)S(1)}, u32[]{:S(2)}, u32[]{:S(2)}) collective-permute-start(f32[3,8,128]{2,1,0:T(8,128)} %get-tuple-element.9), channel_id=1, source_target_pairs={{0,1},{1,2},{2,3},{3,4},{4,5},{5,6},{6,7},{7,8},{8,9},{9,10},{10,1... | collective-permute-start | bytes 36872 | tf_op jit(solution)/shard_map/ppermute | solution.py:436
  5.1 6.0 %collective-permute-start.1 = (f32[3,8,128]{2,1,0:T(8,128)}, f32[3,8,128]{2,1,0:T(8,128)S(1)}, u32[]{:S(2)}, u32[]{:S(2)}) collective-permute-start(f32[3,8,128]{2,1,0:T(8,128)} %get-tuple-element.10), channel_id=1, source_target_pairs={{0,15},{1,0},{2,1},{3,2},{4,3},{5,4},{6,5},{7,6},{8,7},{9,8},{10,9... | collective-permute-start | bytes 36872 | tf_op jit(solution)/shard_map/ppermute | solution.py:437
  9.3 0.9 %copy-start = (f32[3,128,128]{2,1,0:T(8,128)S(1)}, f32[3,128,128]{2,1,0:T(8,128)}, u32[]{:S(2)}) copy-start(f32[3,128,128]{2,1,0:T(8,128)} %get-tuple-element.8.rows_ref) | copy-start | bytes 589828
  11.8 10.3 %copy-start.1 = (f32[4,2]{0,1:T(2,128)S(1)}, f32[4,2]{0,1:T(2,128)}, u32[]{:S(2)}) copy-start(f32[4,2]{0,1:T(2,128)} %param.9) | copy-start | bytes 100
  11.8 27.5 %all-to-all-start = ((f32[32,17,2,128]{3,2,1,0:T(2,128)}), f32[32,17,2,128]{3,2,1,0:T(2,128)S(1)}, u32[]{:S(2)}, u32[]{:S(2)}) async-start(f32[32,17,2,128]{3,2,1,0:T(2,128)} %bitcast), calls=%async_computation | async-start | bytes 1114112 | tf_op jit(solution)/shard_map/all_to_all | solution.py:409
  58.9 16.4 %all-to-all-start.2 = ((f32[16,1,128]{2,1,0:T(1,128)}), f32[16,1,128]{2,1,0:T(1,128)S(1)}, u32[]{:S(2)}, u32[]{:S(2)}) async-start(f32[16,1,128]{2,1,0:T(1,128)} %gaps.1), calls=%async_computation.2 | async-start | bytes 16384 | tf_op jit(solution)/shard_map/all_to_all | solution.py:507
